TPU v7x, 1024 devices: a whole 4x4x32 slice. The times are simulated.
1024 devices in a mesh: bx: 8 (over y, core), by: 8 (over z_hi, x), bz: 16 (over z_lo).
Axes of the slice: x: 4, y: 4, z: 32 (z_hi: 2, z_lo: 16; z = z_hi * 16 + z_lo), core: 2. Of those that a mesh axis runs over, the one named last changes fastest.
Arguments:
- features: bfloat16 [8, 8, 16, 64, 640], P('bx', 'by', 'bz'), may hold values from -5 to 5
- shifts: bfloat16 [8, 8, 16, 64, 3], P('bx', 'by', 'bz'), may hold values from -0.34960938 to 0.34960938
- block_counts: int32 [8, 8, 16], P('bx', 'by', 'bz'), may hold values from 16 to 48, as said below
- block_centres: int32 [8, 8, 16, 48, 4], P('bx', 'by', 'bz'), may hold values from 0 to 511, as said below
- block_neighbours: int32 [8, 8, 16, 48, 128], P('bx', 'by', 'bz'), may hold values from 0 to 511, as said below
- w_pair: bfloat16 [128, 128], replicated, may hold values from -0.5 to 0.5
- w_radial: float32 [8, 128], replicated, may hold values from -2 to 2
- w_mix: bfloat16 [128, 192], replicated, may hold values from -0.5 to 0.5
- w_self: bfloat16 [128, 128], replicated, may hold values from -0.5 to 0.5
- w_tensor: bfloat16 [64, 128], replicated, may hold values from -0.75 to 0.75
- w_out: float32 [128], replicated, may hold values from -0.125 to 0.125
Outputs:
- energies: float32 [8, 8, 16, 64], P('bx', 'by', 'bz')
- forces: float32 [8, 8, 16, 3, 64], P('bx', 'by', 'bz')
Inputs may be any that keep to these rules, and one draw needn't show every extreme that they name: `block_counts`: every draw has boxes with all 48 blocks filled. `block_centres`: A block's 4 centres lie inside the box or in the two lattice layers around it. `block_neighbours`: each edge joins two different lattice sites at most 2 steps apart in each coordinate, at least one of them inside the box; a centre outside the box has only neighbours inside it.
All inputs are finite; a program needn't handle non-finite values.
Results may differ from a plain program's by a relative error of at most 0.015.
Values may be sent and summed in bfloat16 or wider, within the bound.
A program may use at most 32 MiB of HBM per device.

v0:
```python
import functools
import math

import jax
import jax.numpy as jnp
from jax import lax
from jax.experimental import pallas as pl
from jax.experimental.pallas import tpu as pltpu
from jax.sharding import PartitionSpec as P

MESH = pl.DeviceIdType.MESH
F32 = jnp.float32
BF16 = jnp.bfloat16

cutoff_radius = 6.0
site_spacing = 1.7
root_three = math.sqrt(3.0)
root_five = math.sqrt(5.0)
root_fifteen = math.sqrt(15.0)

ROWS = 512
HALF = 256
WIDE = 640
SLIM = 128
BLOCKS = 48
EDGES = 128
PAIRS = BLOCKS // 2
LANES = 2 * EDGES


def phase_two_sends():
    return (
        (0, 1, 32, 64, 32),
        (0, -1, 0, 96, 32),
        (1, 0, 16, 128, 16),
        (1, 0, 48, 144, 16),
        (-1, 0, 0, 160, 16),
        (-1, 0, 32, 176, 16),
        (1, 1, 48, 192, 16),
        (1, -1, 16, 208, 16),
        (-1, 1, 32, 224, 16),
        (-1, -1, 0, 240, 16),
    )


SENDS = len(phase_two_sends())


def wrapped(axis, step):
    size = lax.axis_size(axis)
    return lax.rem(lax.axis_index(axis) + size + step, size)


def at_device(dx, dy, dz):
    return (wrapped("bx", dx), wrapped("by", dy), wrapped("bz", dz))


def octants(rows, order):
    return jnp.concatenate([rows[8 * o : 8 * o + 8] for o in order], axis=0)


def place_own(features_ref, shifts_ref, slim, wide, by_slim_out, by_wide_out, packed):
    packed[...] = jnp.zeros_like(packed)
    packed[:, 0:64] = features_ref[:, 0:64].astype(F32)
    packed[:, 64:67] = shifts_ref[...].astype(F32)
    own = [4 * ox + 2 * oy + oz for oz in range(2) for ox in range(2) for oy in range(2)]
    for source, table, out in (
        (packed[...], slim, by_slim_out),
        (features_ref[...].astype(F32), wide, by_wide_out),
    ):
        table[0:64, :] = octants(source, own).astype(BF16)
        for oy in range(2):
            face = [4 * ox + 2 * oy + oz for oz in range(2) for ox in range(2)]
            out[oy] = octants(source, face).astype(BF16)


def place_halo(table, landed):
    pieces = []
    below, above = landed[0].astype(F32), landed[1].astype(F32)
    for q in range(4):
        pieces += [below[8 * q : 8 * q + 8], above[8 * q : 8 * q + 8]]
    table[HALF : HALF + 64, :] = jnp.concatenate(pieces, axis=0).astype(BF16)


def entry_barrier():
    barrier = pltpu.get_barrier_semaphore()
    partners = [(0, 1, 0), (0, -1, 0)] + [
        (dx, 0, dz) for dx in (-1, 0, 1) for dz in (-1, 0, 1) if dx or dz
    ]
    for dx, dy, dz in partners:
        pl.semaphore_signal(barrier, inc=1, device_id=at_device(dx, dy, dz), device_id_type=MESH)
    pl.semaphore_wait(barrier, len(partners))


def by_copies(out, landed, send_sem, recv_sem):
    return [
        pltpu.make_async_remote_copy(
            src_ref=out.at[1 - side],
            dst_ref=landed.at[side],
            send_sem=send_sem.at[side],
            recv_sem=recv_sem.at[side],
            device_id=at_device(0, 1 - 2 * side, 0),
            device_id_type=MESH,
        )
        for side in range(2)
    ]


def half_copies(table, half, send_sem, recv_sem):
    return [
        pltpu.make_async_remote_copy(
            src_ref=table.at[pl.ds(HALF * half + source, rows)],
            dst_ref=table.at[pl.ds(HALF * half + target, rows)],
            send_sem=send_sem.at[half, at],
            recv_sem=recv_sem.at[half, at],
            device_id=at_device(dx, 0, dz),
            device_id_type=MESH,
        )
        for at, (dx, dz, source, target, rows) in enumerate(phase_two_sends())
    ]


def halo_kernel(
    features_ref,
    shifts_ref,
    slim,
    wide,
    by_slim_out,
    by_wide_out,
    by_slim_in,
    by_wide_in,
    packed,
    by_send,
    by_recv,
    send_sem,
    recv_sem,
):
    place_own(features_ref, shifts_ref, slim, wide, by_slim_out, by_wide_out, packed)
    entry_barrier()
    tables = (
        (slim, by_slim_out, by_slim_in, 0),
        (wide, by_wide_out, by_wide_in, 1),
    )
    by = [by_copies(out, landed, by_send.at[t], by_recv.at[t]) for _, out, landed, t in tables]
    own = [half_copies(table, 0, send_sem.at[t], recv_sem.at[t]) for table, _, _, t in tables]
    far = [half_copies(table, 1, send_sem.at[t], recv_sem.at[t]) for table, _, _, t in tables]
    for t in range(2):
        for copy in by[t]:
            copy.start()
    for t in range(2):
        for copy in own[t]:
            copy.start()
    for table, _, landed, t in tables:
        for copy in by[t]:
            copy.wait()
        place_halo(table, landed)
        for copy in far[t]:
            copy.start()
    for t in range(2):
        for copy in own[t] + far[t]:
            copy.wait()


def dot_nn(left, right):
    return lax.dot_general(left, right, (((1,), (0,)), ((), ())), preferred_element_type=F32)


def dot_nt(left, right):
    return lax.dot_general(left, right, (((1,), (1,)), ((), ())), preferred_element_type=F32)


def split(value):
    high = value.astype(BF16)
    return high, (value - high.astype(F32)).astype(BF16)


def cell_digits(row):
    return row >> 7, (row >> 5) & 3, (row >> 3) & 3, row & 7


def coordinates(row):
    ci, cj, ck, w = cell_digits(row)
    return (
        2 * (ci - 1) + (w >> 2),
        2 * (cj - 1) + ((w >> 1) & 1),
        2 * (ck - 1) + (w & 1),
    )


def table_row(row):
    ci, cj, ck, w = cell_digits(row)
    ox, oz = ci - 1, ck - 1
    inner_x = (ci == 1) | (ci == 2)
    inner_y = (cj == 1) | (cj == 2)
    inner_z = (ck == 1) | (ck == 2)
    x_side, z_side = ci >> 1, ck >> 1
    base = jnp.where(
        inner_x,
        jnp.where(inner_z, 32 * oz + 16 * ox, 64 + 32 * z_side + 16 * ox),
        jnp.where(inner_z, 128 + 32 * x_side + 16 * oz, 192 + 32 * x_side + 16 * z_side),
    )
    y_part = jnp.where(inner_y, 8 * (cj - 1), HALF + 8 * (cj >> 1))
    return base + y_part + w


def inner_atom(row):
    ci, cj, ck, w = cell_digits(row)
    inside = (ci == 1) | (ci == 2)
    inside = inside & ((cj == 1) | (cj == 2)) & ((ck == 1) | (ck == 2))
    return jnp.where(inside, 8 * (4 * (ci - 1) + 2 * (cj - 1) + ck - 1) + w, -1)


def lane_slot(shape):
    return lax.broadcasted_iota(jnp.int32, shape, 1) >> 5


def over_edges(columns, slots):
    spread = [jnp.broadcast_to(column, slots.shape) for column in columns]
    low = jnp.where(slots == 0, spread[0], spread[1])
    high = jnp.where(slots == 2, spread[2], spread[3])
    return jnp.where(slots < 2, low, high)


def slot_mask():
    slots = lane_slot((8, LANES))
    return jnp.where(slots == lax.broadcasted_iota(jnp.int32, (8, LANES), 0), 1.0, 0.0).astype(F32)


def edges_kernel(
    slim,
    wide,
    count_ref,
    centres_ref,
    neighbours_ref,
    w_pair_ref,
    w_radial_ref,
    w_mix_ref,
    w_self_ref,
    w_tensor_ref,
    w_out_ref,
    energies_ref,
    forces_ref,
    scratch,
):
    (
        turned,
        spots,
        scalars,
        shift_rows,
        centre_slim,
        centre_wide,
        basis_rows,
        sphere_rows,
        back_rows,
        pulled,
    ) = scratch

    turned[...] = slim[...].astype(F32).T[0:80].astype(BF16)

    neighbours = neighbours_ref[...]
    centres = centres_ref[...]
    spots[...] = table_row(neighbours)
    centre_spots = table_row(centres)

    centre_shift = []
    lanes_of_rows = lax.broadcasted_iota(jnp.int32, (BLOCKS, ROWS), 1)
    for place in range(4):
        hits = jnp.where(centre_spots[:, place : place + 1] == lanes_of_rows, 1.0, 0.0).astype(BF16)
        got = dot_nn(hits, slim[...])
        centre_slim[pl.ds(place, BLOCKS, stride=4), :] = got
        centre_shift.append([got[:, 64 + axis : 65 + axis] for axis in range(3)])
        got = dot_nn(hits, wide[...])
        for at in range(WIDE // 128):
            centre_wide[at, pl.ds(place, BLOCKS, stride=4), :] = got[:, 128 * at : 128 * at + 128]

    def gather(pair, _):
        hits = []
        rows = lax.broadcasted_iota(jnp.int32, (ROWS, EDGES), 0).astype(jnp.int16)
        for block in range(2):
            spot = spots[pl.ds(2 * pair + block, 1), :].astype(jnp.int16)
            hits.append(
                jnp.where(rows == spot, jnp.ones((), BF16), jnp.zeros((), BF16))
            )
        got = dot_nn(turned[...], jnp.concatenate(hits, axis=1))
        scalars[pair] = got[0:64].astype(BF16)
        for block in range(2):
            shift_rows[pl.ds(pl.multiple_of((2 * pair + block) * 8, 8), 8), :] = got[
                64:72, EDGES * block : EDGES * block + EDGES
            ]
        return 0

    lax.fori_loop(0, PAIRS, gather, 0)

    slots = lane_slot((BLOCKS, EDGES))
    centre_rows = over_edges([centres[:, j : j + 1] for j in range(4)], slots)
    vector = []
    for axis, (one, other) in enumerate(zip(coordinates(neighbours), coordinates(centre_rows))):
        near = shift_rows[pl.ds(axis, BLOCKS, stride=8), :]
        far = over_edges([centre_shift[j][axis] for j in range(4)], slots)
        vector.append((one - other).astype(F32) * site_spacing + (near - far))
    distance = jnp.sqrt(vector[0] * vector[0] + vector[1] * vector[1] + vector[2] * vector[2])
    inverse = 1.0 / distance
    ux, uy, uz = [part * inverse for part in vector]
    inside = distance < cutoff_radius
    scaled = jnp.minimum(distance * (1.0 / cutoff_radius), 1.0)
    fifth = (scaled * scaled) * (scaled * scaled) * scaled
    envelope = 1.0 - fifth * scaled * (28.0 - scaled * (48.0 - 21.0 * scaled))
    envelope_slope = jnp.where(
        inside, fifth * (-168.0 + scaled * (336.0 - 168.0 * scaled)) * (1.0 / cutoff_radius), 0.0
    )
    sine, cosine = jnp.sin(math.pi * scaled), jnp.cos(math.pi * scaled)
    norm = math.sqrt(2.0 / cutoff_radius) * inverse
    cut_norm = norm * envelope
    slope_sine = norm * (envelope_slope - envelope * inverse)
    slope_cosine = jnp.where(inside, cut_norm * (math.pi / cutoff_radius), 0.0)
    sines, cosines = [sine], [cosine]
    for _ in range(7):
        s, c = sines[-1], cosines[-1]
        sines.append(s * cosine + c * sine)
        cosines.append(c * cosine - s * sine)
    for k in range(8):
        basis_rows[pl.ds(k, BLOCKS, stride=8), :] = sines[k] * cut_norm
    sphere = (
        root_three * ux,
        root_three * uy,
        root_three * uz,
        root_fifteen * ux * uy,
        root_fifteen * uy * uz,
        0.5 * root_five * (3.0 * uz * uz - 1.0),
        root_fifteen * ux * uz,
        0.5 * root_fifteen * (ux * ux - uy * uy),
    )
    for m in range(8):
        sphere_rows[pl.ds(m, BLOCKS, stride=8), :] = sphere[m]

    mask = slot_mask()
    mask_b = mask.astype(BF16)
    w_pair = w_pair_ref[...]
    centre_part = dot_nn(
        centre_slim[:, 0:64].astype(BF16), w_pair[0:64]
    )
    centre_slim[...] = centre_part
    radial = w_radial_ref[...]
    radial_high, radial_low = split(radial)
    radial_rows = jnp.concatenate([radial_high.astype(F32), radial_low.astype(F32)], axis=0).astype(BF16)
    w_mix = w_mix_ref[...].astype(F32)
    mix_turned = w_mix.T
    mix_turned = jnp.concatenate(
        [mix_turned[128:192], mix_turned[64:128], mix_turned[0:64]], axis=0
    )
    mix_back = mix_turned.T.astype(BF16)
    mix_turned = mix_turned.astype(BF16)
    update = jnp.concatenate([w_self_ref[...], w_tensor_ref[...]], axis=0)
    update_turned = update.astype(F32).T.astype(BF16)
    w_out = jnp.broadcast_to(w_out_ref[...].astype(F32), (128, 128)).T
    w_out = jnp.concatenate([w_out, w_out], axis=1)
    low_half = lax.broadcasted_iota(jnp.int32, (8, 128), 1) < 64
    nothing = jnp.zeros((8, 128), F32)

    group = 4

    def latents(pair):
        at = pl.multiple_of(8 * pair, 8)
        high, low = split(centre_slim[pl.ds(at, 8), :])
        left = jnp.concatenate(
            [
                w_pair[64:128].astype(F32),
                high.astype(F32),
                low.astype(F32),
                radial_high.astype(F32),
                radial_high.astype(F32),
                radial_low.astype(F32),
                jnp.zeros((24, 128), F32),
            ],
            axis=0,
        ).T.astype(BF16)
        at = pl.multiple_of(16 * pair, 16)
        basis = jnp.concatenate(
            [basis_rows[pl.ds(at, 8), :], basis_rows[pl.ds(at + 8, 8), :]], axis=1
        )
        high, low = split(basis)
        right = jnp.concatenate(
            [mask, mask, high.astype(F32), low.astype(F32), high.astype(F32), jnp.zeros((24, LANES), F32)],
            axis=0,
        ).astype(BF16)
        return dot_nn(left, jnp.concatenate([scalars[pair], right], axis=0))

    def tensors(pair):
        at = pl.multiple_of(8 * pair, 8)
        parts = [centre_wide[g, pl.ds(at, 8), :] for g in range(5)]
        turns = [pltpu.roll(part, 64, 1) for part in parts]
        order_one = [turns[1], parts[1], turns[2]]
        order_two = [turns[2], parts[3], turns[3], parts[4], turns[4]]
        rows = [jnp.where(low_half, 0.0, part) for part in order_one]
        rows += [jnp.where(low_half, part, 0.0) for part in order_two]
        back = jnp.concatenate(rows, axis=0)
        zero = jnp.where(low_half, turns[0], 0.0)
        first = jnp.concatenate([back, nothing, nothing], axis=0).T
        second = jnp.concatenate([nothing] * 8 + [zero, nothing], axis=0).T[0:64]
        front = jnp.concatenate([first, second], axis=0)
        return front.astype(BF16), back.astype(BF16)

    def spheres(pair):
        at = pl.multiple_of(16 * pair, 16)
        sphere = jnp.concatenate(
            [sphere_rows[pl.ds(at, 8), :], sphere_rows[pl.ds(at + 8, 8), :]], axis=1
        )
        rows = [jnp.broadcast_to(sphere[m : m + 1], (8, LANES)) * mask for m in range(8)]
        return jnp.concatenate(rows + [mask, jnp.zeros((8, LANES), F32)], axis=0).astype(BF16)

    def silu_parts(x):
        gate = 0.5 * jnp.tanh(0.5 * x) + 0.5
        value = x * gate
        return value, gate + value * (1.0 - gate)

    def one_group(turn, _):
        pairs = [turn * group + g for g in range(group)]
        each = range(group)
        x1 = [latents(p) for p in pairs]
        sides = [tensors(p) for p in pairs]
        contracted = [dot_nn(sides[g][0], spheres(pairs[g])) for g in each]
        first = [silu_parts(x) for x in x1]
        latent = [value.astype(BF16) for value, _ in first]
        mixing = [dot_nn(mix_turned, value) for value in latent]
        coupled = []
        for g in each:
            product = mixing[g] * contracted[g]
            coupled.append((product[0:64] + product[64:128] + product[128:192]).astype(BF16))
        hidden_in = [
            dot_nn(update_turned, jnp.concatenate([latent[g], coupled[g]], axis=0)) for g in each
        ]
        second = [silu_parts(x) for x in hidden_in]
        readout = [jnp.sum(value * w_out, axis=0, keepdims=True) for value, _ in second]
        back = [dot_nn(update, (slope * w_out).astype(BF16)) for _, slope in second]
        for g in each:
            cotangent = back[g][128:192].astype(BF16).astype(F32)
            cotangents = jnp.concatenate([cotangent, cotangent, cotangent], axis=0)
            to_mixing = (cotangents * contracted[g]).astype(BF16)
            to_contracted = (cotangents[0:128] * mixing[g][0:128]).astype(BF16)
            to_latent = back[g][0:128] + dot_nn(mix_back, to_mixing)
            to_sphere = dot_nn(sides[g][1], to_contracted)
            to_sphere = jnp.sum(to_sphere.reshape(8, 8, LANES) * mask[None], axis=1)
            to_input = (to_latent * first[g][1]).astype(BF16)
            to_basis = dot_nn(radial_rows, to_input)
            to_basis = to_basis[0:8] + to_basis[8:16]
            for block in range(2):
                at = (2 * pairs[g] + block) * 24
                lanes = slice(EDGES * block, EDGES * block + EDGES)
                back_rows[pl.ds(pl.multiple_of(at, 8), 8), :] = to_sphere[:, lanes]
                back_rows[pl.ds(pl.multiple_of(at + 8, 8), 8), :] = to_basis[:, lanes]
                back_rows[pl.ds(pl.multiple_of(at + 16, 8), 8), :] = jnp.broadcast_to(
                    readout[g][:, lanes], (8, EDGES)
                )
        return 0

    lax.fori_loop(0, PAIRS // group, one_group, 0)

    def backs(row):
        return back_rows[pl.ds(row, BLOCKS, stride=24), :]

    count = count_ref[...]
    active = lax.broadcasted_iota(jnp.int32, (BLOCKS, EDGES), 0) < count
    readout = backs(16)
    energy = jnp.where(active, envelope * readout, 0.0)
    radial_pull = envelope_slope * readout
    along_sine, along_cosine = 0.0, 0.0
    for k in range(8):
        to_basis = backs(8 + k)
        along_sine = along_sine + to_basis * sines[k]
        along_cosine = along_cosine + to_basis * (cosines[k] * (k + 1.0))
    radial_pull = radial_pull + envelope * (along_sine * slope_sine + along_cosine * slope_cosine)
    y1, y2, y3, y4, y5, y6, y7, y8 = [backs(m) for m in range(8)]
    gx = root_three * y1 + root_fifteen * (uy * y4 + uz * y7 + ux * y8)
    gy = root_three * y2 + root_fifteen * (ux * y4 + uz * y5 - uy * y8)
    gz = root_three * y3 + root_fifteen * (uy * y5 + ux * y7) + (3.0 * root_five) * uz * y6
    turn_norm = envelope * inverse
    radial_pull = radial_pull - turn_norm * (gx * ux + gy * uy + gz * uz)
    pulls = [
        jnp.where(active, radial_pull * u + turn_norm * g, 0.0)
        for u, g in ((ux, gx), (uy, gy), (uz, gz))
    ]
    pulled[...] = jnp.zeros_like(pulled)
    for at, value in enumerate(pulls + [energy]):
        high, low = split(value)
        low_low = value - high.astype(F32) - low.astype(F32)
        for part, piece in enumerate((high.astype(F32), low.astype(F32), low_low)):
            pulled[pl.ds(4 * part + at, BLOCKS, stride=16), :] = piece
    near_atom = inner_atom(neighbours)
    far_atom = inner_atom(centre_rows)
    spots[...] = near_atom
    shift_rows[0:BLOCKS, :] = far_atom.astype(F32)

    def scatter(block, totals):
        atoms = lax.broadcasted_iota(jnp.int32, (64, EDGES), 0)
        near = jnp.where(atoms == spots[pl.ds(block, 1), :], 1.0, 0.0)
        far = jnp.where(atoms == shift_rows[pl.ds(block, 1), :].astype(jnp.int32), 1.0, 0.0)
        values = pulled[pl.ds(pl.multiple_of(16 * block, 16), 16), :].astype(BF16)
        return (
            totals[0] + dot_nt(values, (far - near).astype(BF16)),
            totals[1] + dot_nt(values, far.astype(BF16)),
        )

    start = jnp.zeros((16, 64), F32)
    force, energy = lax.fori_loop(0, BLOCKS, scatter, (start, start))
    forces_ref[...] = force[0:3] + force[4:7] + force[8:11]
    energies_ref[...] = energy[3:4] + energy[7:8] + energy[11:12]


def edge_scratch():
    return [
        pltpu.VMEM((80, ROWS), BF16),
        pltpu.VMEM((BLOCKS, EDGES), jnp.int32),
        pltpu.VMEM((PAIRS, 64, LANES), BF16),
        pltpu.VMEM((8 * BLOCKS, EDGES), F32),
        pltpu.VMEM((4 * BLOCKS, SLIM), F32),
        pltpu.VMEM((WIDE // 128, 4 * BLOCKS, 128), F32),
        pltpu.VMEM((8 * BLOCKS, EDGES), F32),
        pltpu.VMEM((8 * BLOCKS, EDGES), F32),
        pltpu.VMEM((24 * BLOCKS, EDGES), F32),
        pltpu.VMEM((16 * BLOCKS, EDGES), F32),
    ]


VMEM = pl.BlockSpec(memory_space=pltpu.VMEM)


def halo(features, shifts):
    return pl.pallas_call(
        halo_kernel,
        out_shape=(
            jax.ShapeDtypeStruct((ROWS, SLIM), BF16),
            jax.ShapeDtypeStruct((ROWS, WIDE), BF16),
        ),
        in_specs=[VMEM, VMEM],
        out_specs=(VMEM, VMEM),
        scratch_shapes=[
            pltpu.VMEM((2, 32, SLIM), BF16),
            pltpu.VMEM((2, 32, WIDE), BF16),
            pltpu.VMEM((2, 32, SLIM), BF16),
            pltpu.VMEM((2, 32, WIDE), BF16),
            pltpu.VMEM((64, SLIM), F32),
            pltpu.SemaphoreType.DMA((2, 2)),
            pltpu.SemaphoreType.DMA((2, 2)),
            pltpu.SemaphoreType.DMA((2, 2, SENDS)),
            pltpu.SemaphoreType.DMA((2, 2, SENDS)),
        ],
        compiler_params=pltpu.CompilerParams(
            collective_id=0, has_side_effects=True, vmem_limit_bytes=32 * 2**20
        ),
        name="halo",
    )(features, shifts)


def edges(slim, wide, *rest):
    def kernel(*refs):
        edges_kernel(*refs[:13], refs[13:])

    return pl.pallas_call(
        kernel,
        out_shape=(
            jax.ShapeDtypeStruct((1, 64), F32),
            jax.ShapeDtypeStruct((3, 64), F32),
        ),
        in_specs=[VMEM] * 11,
        out_specs=(VMEM, VMEM),
        scratch_shapes=edge_scratch(),
        compiler_params=pltpu.CompilerParams(vmem_limit_bytes=48 * 2**20),
        name="edges",
    )(slim, wide, *rest)


def per_device(
    features,
    shifts,
    block_counts,
    block_centres,
    block_neighbours,
    w_pair,
    w_radial,
    w_mix,
    w_self,
    w_tensor,
    w_out,
):
    slim, wide = halo(features.reshape(64, WIDE), shifts.reshape(64, 3))
    energies, forces = edges(
        slim,
        wide,
        block_counts.reshape(1, 1),
        block_centres.reshape(BLOCKS, 4),
        block_neighbours.reshape(BLOCKS, EDGES),
        w_pair,
        w_radial,
        w_mix,
        w_self,
        w_tensor,
        w_out.reshape(1, 128),
    )
    return energies.reshape(1, 1, 1, 64), forces.reshape(1, 1, 1, 3, 64)


def solution(mesh):
    in_specs = (
        P("bx", "by", "bz", None, None),
        P("bx", "by", "bz", None, None),
        P("bx", "by", "bz"),
        P("bx", "by", "bz", None, None),
        P("bx", "by", "bz", None, None),
        P(),
        P(),
        P(),
        P(),
        P(),
        P(),
    )
    out_specs = (P("bx", "by", "bz", None), P("bx", "by", "bz", None, None))
    return jax.shard_map(
        per_device, mesh=mesh, in_specs=in_specs, out_specs=out_specs, check_vma=False
    )
```

profile of v0, /device:TPU:1, one launch (start us, length us, event | category | flops | bytes accessed | tf_op | source)
XLA Modules:
  0.0 88.0 jit_solution(7490028473614437974)
XLA Ops:
  0.6 0.8 copy.13
  1.4 0.0 copy-start
  1.4 0.9 %copy-done = bf16[1,1,1,64,640]{4,3,2,1,0:T(8,128)(2,1)S(1)} copy-done((bf16[1,1,1,64,640]{4,3,2,1,0:T(8,128)(2,1)S(1)}, bf16[1,1,1,64,640]{4,3,2,1,0:T(8,128)(2,1)}, u32[]{:S(2)}) %copy-start) | copy-done | bytes 81944
  2.3 0.0 copy-start.7
  2.3 59.6 %halo.1 = (bf16[512,128]{1,0:T(8,128)(2,1)S(1)}, bf16[512,640]{1,0:T(8,128)(2,1)S(1)}) custom-call(bf16[64,640]{1,0:T(8,128)(2,1)S(1)} %bitcast.10, bf16[64,3]{1,0:T(8,128)(2,1)S(1)} %bitcast.11), custom_call_target="tpu_custom_call" | custom-call | tf_op jit(solution)/shard_map/halo/pallas_call | solution.py:528
  61.9 0.0 copy-done.7
  62.0 0.0 copy-start.8
  62.0 0.0 copy-start.2
  62.0 0.0 copy-start.3
  62.0 0.0 copy-start.4
  62.0 0.0 copy-start.5
  62.0 0.1 copy.15.refs_7_
  62.1 0.5 copy-done.8
  62.6 0.0 copy-start.1
  62.6 0.1 copy.14
  63.4 0.0 copy-start.6
  63.4 0.0 copy-done.2
  63.4 0.0 copy-done.3
  63.4 0.0 copy-done.4
  63.4 0.0 copy-done.5
  63.4 0.0 copy-done.1
  63.4 0.6 copy-done.6
  64.0 23.3 %edges.1 = (f32[1,64]{1,0:T(1,128)}, f32[3,64]{1,0:T(4,128)S(1)}) custom-call(bf16[512,128]{1,0:T(8,128)(2,1)S(1)} %get-tuple-element.6.refs_0_, bf16[512,640]{1,0:T(8,128)(2,1)S(1)} %get-tuple-element.7.refs_1_, s32[1,1]{1,0:T(1,128)} %bitcast.8.refs_2_, s32[48,4]{1,0:T(8,128)S(1)} %bitcast.9, s32[48,128]{1,0:T(8,128)S(1)} %bitcast.12, ...), custom_call_target="tpu_custom_call" | custom-call | tf_op jit(solution)/shard_map/edges/pallas_call | solution.py:558
  87.4 0.6 copy.16
Async XLA Ops:
  1.4 0.9 %copy-start = (bf16[1,1,1,64,640]{4,3,2,1,0:T(8,128)(2,1)S(1)}, bf16[1,1,1,64,640]{4,3,2,1,0:T(8,128)(2,1)}, u32[]{:S(2)}) copy-start(bf16[1,1,1,64,640]{4,3,2,1,0:T(8,128)(2,1)} %param.11) | copy-start | bytes 245764
  2.3 59.6 %copy-start.7 = (bf16[128,192]{0,1:T(8,128)(2,1)S(1)}, bf16[128,192]{0,1:T(8,128)(2,1)}, u32[]{:S(2)}) copy-start(bf16[128,192]{0,1:T(8,128)(2,1)} %param.18) | copy-start | bytes 147460
  62.0 0.7 copy-start.8
  62.0 1.4 %copy-start.2 = (bf16[128,128]{1,0:T(8,128)(2,1)S(1)}, bf16[128,128]{1,0:T(8,128)(2,1)}, u32[]{:S(2)}) copy-start(bf16[128,128]{1,0:T(8,128)(2,1)} %refs_8_.1) | copy-start | bytes 98308
  62.0 1.4 %copy-start.3 = (s32[1,1,1,48,128]{4,3,2,1,0:T(8,128)S(1)}, s32[1,1,1,48,128]{4,3,2,1,0:T(8,128)}, u32[]{:S(2)}) copy-start(s32[1,1,1,48,128]{4,3,2,1,0:T(8,128)} %param.15) | copy-start | bytes 73732
  62.0 1.4 %copy-start.4 = (bf16[64,128]{1,0:T(8,128)(2,1)S(1)}, bf16[64,128]{1,0:T(8,128)(2,1)}, u32[]{:S(2)}) copy-start(bf16[64,128]{1,0:T(8,128)(2,1)} %refs_9_.1) | copy-start | bytes 49156
  62.0 1.4 %copy-start.5 = (f32[8,128]{1,0:T(8,128)S(1)}, f32[8,128]{1,0:T(8,128)}, u32[]{:S(2)}) copy-start(f32[8,128]{1,0:T(8,128)} %refs_6_.1) | copy-start | bytes 12292
  62.6 0.8 copy-start.1
  63.4 0.7 copy-start.6
where the time goes:
time: 88.3 us; the launch traced here: 88 us
  Pallas kernels  83 us (94%)
  local copies, waits for them, and re-layouts  3.58 us (4%)
  between operations  1.4 us (2%)
    pallas_call x1, Pallas kernels, halo(): pl.pallas_call(halo_kernel, out_shape=(jax.ShapeDtypeStruct((ROWS, SLIM),...  59.6 us
    pallas_call x1, Pallas kernels, edges(): pl.pallas_call(kernel, out_shape=(jax.ShapeDtypeStruct((1, 64), F32), jax...  23.3 us
    unnamed x22, local copies, waits for them, and re-layouts  3.58 us

commit v1 on v0

--- a/solution.py
+++ b/solution.py
@@ -1,4 +1,3 @@
-import functools
 import math
 
 import jax
@@ -25,6 +24,10 @@
 BLOCKS = 48
 EDGES = 128
 PAIRS = BLOCKS // 2
+SCATTER = 24
+GATHER = 12
+FIRST = 12
+SECOND = 8
 LANES = 2 * EDGES
 
 
@@ -74,91 +77,208 @@
             out[oy] = octants(source, face).astype(BF16)
 
 
-def place_halo(table, landed):
+def place_octants(table, first, landed, count):
     pieces = []
     below, above = landed[0].astype(F32), landed[1].astype(F32)
-    for q in range(4):
+    for q in range(count):
         pieces += [below[8 * q : 8 * q + 8], above[8 * q : 8 * q + 8]]
-    table[HALF : HALF + 64, :] = jnp.concatenate(pieces, axis=0).astype(BF16)
-
-
-def entry_barrier():
+    table[first : first + 16 * count, :] = jnp.concatenate(pieces, axis=0).astype(BF16)
+
+
+def low_wrap():
+    return lax.axis_index("bz") == 0
+
+
+def high_wrap():
+    return lax.axis_index("bz") == lax.axis_size("bz") - 1
+
+
+def greet():
     barrier = pltpu.get_barrier_semaphore()
     partners = [(0, 1, 0), (0, -1, 0)] + [
         (dx, 0, dz) for dx in (-1, 0, 1) for dz in (-1, 0, 1) if dx or dz
     ]
-    for dx, dy, dz in partners:
+
+    def signal(dx, dy, dz):
         pl.semaphore_signal(barrier, inc=1, device_id=at_device(dx, dy, dz), device_id_type=MESH)
-    pl.semaphore_wait(barrier, len(partners))
-
-
-def by_copies(out, landed, send_sem, recv_sem):
-    return [
-        pltpu.make_async_remote_copy(
-            src_ref=out.at[1 - side],
-            dst_ref=landed.at[side],
-            send_sem=send_sem.at[side],
-            recv_sem=recv_sem.at[side],
-            device_id=at_device(0, 1 - 2 * side, 0),
+
+    for wraps, dz in ((low_wrap, -1), (high_wrap, 1)):
+
+        @pl.when(wraps())
+        def _():
+            signal(0, 1, dz)
+            signal(0, -1, dz)
+
+    for partner in partners:
+        signal(*partner)
+    return len(partners)
+
+
+def meet(count):
+    ends = jnp.where(low_wrap() | high_wrap(), 2, 0)
+    pl.semaphore_wait(pltpu.get_barrier_semaphore(), count + ends)
+
+
+class Exchange:
+    def __init__(self, table, out, landed, corner, by_send, by_recv, send, recv):
+        self.table, self.out, self.landed, self.corner = table, out, landed, corner
+        self.by_send, self.by_recv, self.send, self.recv = by_send, by_recv, send, recv
+
+    def copy(self, source, target, send, recv, dx, dy, dz):
+        return pltpu.make_async_remote_copy(
+            src_ref=source,
+            dst_ref=target,
+            send_sem=send,
+            recv_sem=recv,
+            device_id=at_device(dx, dy, dz),
             device_id_type=MESH,
         )
-        for side in range(2)
-    ]
-
-
-def half_copies(table, half, send_sem, recv_sem):
-    return [
-        pltpu.make_async_remote_copy(
-            src_ref=table.at[pl.ds(HALF * half + source, rows)],
-            dst_ref=table.at[pl.ds(HALF * half + target, rows)],
-            send_sem=send_sem.at[half, at],
-            recv_sem=recv_sem.at[half, at],
-            device_id=at_device(dx, 0, dz),
-            device_id_type=MESH,
-        )
-        for at, (dx, dz, source, target, rows) in enumerate(phase_two_sends())
-    ]
-
-
-def halo_kernel(
-    features_ref,
-    shifts_ref,
-    slim,
-    wide,
-    by_slim_out,
-    by_wide_out,
-    by_slim_in,
-    by_wide_in,
-    packed,
-    by_send,
-    by_recv,
-    send_sem,
-    recv_sem,
-):
-    place_own(features_ref, shifts_ref, slim, wide, by_slim_out, by_wide_out, packed)
-    entry_barrier()
-    tables = (
-        (slim, by_slim_out, by_slim_in, 0),
-        (wide, by_wide_out, by_wide_in, 1),
-    )
-    by = [by_copies(out, landed, by_send.at[t], by_recv.at[t]) for _, out, landed, t in tables]
-    own = [half_copies(table, 0, send_sem.at[t], recv_sem.at[t]) for table, _, _, t in tables]
-    far = [half_copies(table, 1, send_sem.at[t], recv_sem.at[t]) for table, _, _, t in tables]
-    for t in range(2):
-        for copy in by[t]:
+
+    def by_copies(self):
+        return [
+            self.copy(
+                self.out.at[1 - side],
+                self.landed.at[side],
+                self.by_send.at[side],
+                self.by_recv.at[side],
+                0,
+                1 - 2 * side,
+                0,
+            )
+            for side in range(2)
+        ]
+
+    def corner_copies(self, dz):
+        source = 16 if dz > 0 else 0
+        return [
+            self.copy(
+                self.out.at[1 - side, pl.ds(source, 16)],
+                self.corner.at[side],
+                self.by_send.at[2 + side],
+                self.by_recv.at[2 + side],
+                0,
+                1 - 2 * side,
+                dz,
+            )
+            for side in range(2)
+        ]
+
+    def half_copies(self, half):
+        return [
+            (
+                self.copy(
+                    self.table.at[pl.ds(HALF * half + source, rows)],
+                    self.table.at[pl.ds(HALF * half + target, rows)],
+                    self.send.at[half, at],
+                    self.recv.at[half, at],
+                    dx,
+                    0,
+                    dz,
+                ),
+                dz,
+            )
+            for at, (dx, dz, source, target, rows) in enumerate(phase_two_sends())
+        ]
+
+    def late_copies(self, high):
+        piece = HALF + (96 if high else 64)
+        return [
+            self.copy(
+                self.table.at[pl.ds(piece + 16, 16)],
+                self.table.at[pl.ds(HALF + 192 + 16 * high, 16)],
+                self.send.at[2, 0],
+                self.recv.at[2, 0],
+                1,
+                0,
+                0,
+            ),
+            self.copy(
+                self.table.at[pl.ds(piece, 16)],
+                self.table.at[pl.ds(HALF + 224 + 16 * high, 16)],
+                self.send.at[2, 1],
+                self.recv.at[2, 1],
+                -1,
+                0,
+                0,
+            ),
+        ]
+
+    def start_far(self):
+        for copy in self.by_copies():
             copy.start()
-    for t in range(2):
-        for copy in own[t]:
+        for wraps, dz in ((low_wrap, -1), (high_wrap, 1)):
+
+            @pl.when(wraps())
+            def _():
+                for copy in self.corner_copies(dz):
+                    copy.start()
+
+    def start_own(self):
+        for copy, _ in self.half_copies(0):
             copy.start()
-    for table, _, landed, t in tables:
-        for copy in by[t]:
-            copy.wait()
-        place_halo(table, landed)
-        for copy in far[t]:
-            copy.start()
-    for t in range(2):
-        for copy in own[t] + far[t]:
-            copy.wait()
+
+    def pass_on(self):
+        for copy in self.by_copies():
+            copy.wait_recv()
+        place_octants(self.table, HALF, self.landed, 4)
+        for copy, dz in self.half_copies(1):
+            if dz == 0:
+                copy.start()
+            else:
+
+                @pl.when(jnp.logical_not(high_wrap() if dz > 0 else low_wrap()))
+                def _():
+                    copy.start()
+
+        for wraps, dz in ((low_wrap, -1), (high_wrap, 1)):
+
+            @pl.when(wraps())
+            def _():
+                for copy in self.corner_copies(dz):
+                    copy.wait_recv()
+                place_octants(self.table, HALF + (64 if dz < 0 else 96), self.corner, 2)
+                for copy in self.late_copies(int(dz > 0)):
+                    copy.start()
+
+    def arrive(self):
+        for copy, _ in self.half_copies(0):
+            copy.wait_recv()
+        for copy, dz in self.half_copies(1):
+            if dz == 0:
+                copy.wait_recv()
+            else:
+
+                @pl.when(jnp.logical_not(low_wrap() if dz > 0 else high_wrap()))
+                def _():
+                    copy.wait_recv()
+
+        for wraps, high in ((low_wrap, 0), (high_wrap, 1)):
+
+            @pl.when(wraps())
+            def _():
+                for copy in self.late_copies(high):
+                    copy.wait_recv()
+
+    def close(self):
+        for copy in self.by_copies():
+            copy.wait_send()
+        for copy, _ in self.half_copies(0):
+            copy.wait_send()
+        for copy, dz in self.half_copies(1):
+            if dz == 0:
+                copy.wait_send()
+            else:
+
+                @pl.when(jnp.logical_not(high_wrap() if dz > 0 else low_wrap()))
+                def _():
+                    copy.wait_send()
+
+        for wraps, high in ((low_wrap, 0), (high_wrap, 1)):
+
+            @pl.when(wraps())
+            def _():
+                for copy in self.corner_copies(2 * high - 1) + self.late_copies(high):
+                    copy.wait_send()
 
 
 def dot_nn(left, right):
@@ -226,7 +346,10 @@
     return jnp.where(slots == lax.broadcasted_iota(jnp.int32, (8, LANES), 0), 1.0, 0.0).astype(F32)
 
 
-def edges_kernel(
+def edge_work(
+    stop,
+    slim_ready,
+    wide_ready,
     slim,
     wide,
     count_ref,
@@ -240,27 +363,55 @@
     w_out_ref,
     energies_ref,
     forces_ref,
-    scratch,
+    turned,
+    spots,
+    scalars,
+    shift_rows,
+    centre_slim,
+    centre_wide,
+    basis_rows,
+    sphere_rows,
+    back_rows,
+    pulled,
+    far_spots,
+    latent_rows,
+    slope_rows,
+    mixing_rows,
 ):
-    (
-        turned,
-        spots,
-        scalars,
-        shift_rows,
-        centre_slim,
-        centre_wide,
-        basis_rows,
-        sphere_rows,
-        back_rows,
-        pulled,
-    ) = scratch
-
-    turned[...] = slim[...].astype(F32).T[0:80].astype(BF16)
-
     neighbours = neighbours_ref[...]
     centres = centres_ref[...]
     spots[...] = table_row(neighbours)
     centre_spots = table_row(centres)
+    slots = lane_slot((BLOCKS, EDGES))
+    centre_rows = over_edges([centres[:, j : j + 1] for j in range(4)], slots)
+    steps = [
+        (one - other).astype(F32) * site_spacing
+        for one, other in zip(coordinates(neighbours), coordinates(centre_rows))
+    ]
+    mask = slot_mask()
+    w_pair = w_pair_ref[...]
+    radial = w_radial_ref[...]
+    radial_high, radial_low = split(radial)
+    radial_rows = jnp.concatenate([radial_high.astype(F32), radial_low.astype(F32)], axis=0).astype(BF16)
+    w_mix = w_mix_ref[...].astype(F32)
+    mix_turned = w_mix.T
+    mix_turned = jnp.concatenate(
+        [mix_turned[128:192], mix_turned[64:128], mix_turned[0:64]], axis=0
+    )
+    mix_back = mix_turned.T.astype(BF16)
+    mix_turned = mix_turned.astype(BF16)
+    update = jnp.concatenate([w_self_ref[...], w_tensor_ref[...]], axis=0)
+    update_turned = update.astype(F32).T.astype(BF16)
+    w_out = jnp.broadcast_to(w_out_ref[...].astype(F32), (128, 128)).T
+    w_out = jnp.concatenate([w_out, w_out], axis=1)
+    low_half = lax.broadcasted_iota(jnp.int32, (8, 128), 1) < 64
+    nothing = jnp.zeros((8, 128), F32)
+
+    slim_ready()
+    if stop == 0:
+        return
+
+    turned[...] = slim[...].astype(F32).T[0:80].astype(BF16)
 
     centre_shift = []
     lanes_of_rows = lax.broadcasted_iota(jnp.int32, (BLOCKS, ROWS), 1)
@@ -269,35 +420,32 @@
         got = dot_nn(hits, slim[...])
         centre_slim[pl.ds(place, BLOCKS, stride=4), :] = got
         centre_shift.append([got[:, 64 + axis : 65 + axis] for axis in range(3)])
-        got = dot_nn(hits, wide[...])
-        for at in range(WIDE // 128):
-            centre_wide[at, pl.ds(place, BLOCKS, stride=4), :] = got[:, 128 * at : 128 * at + 128]
-
-    def gather(pair, _):
-        hits = []
+
+    def gather(turn, _):
         rows = lax.broadcasted_iota(jnp.int32, (ROWS, EDGES), 0).astype(jnp.int16)
-        for block in range(2):
-            spot = spots[pl.ds(2 * pair + block, 1), :].astype(jnp.int16)
-            hits.append(
-                jnp.where(rows == spot, jnp.ones((), BF16), jnp.zeros((), BF16))
-            )
-        got = dot_nn(turned[...], jnp.concatenate(hits, axis=1))
-        scalars[pair] = got[0:64].astype(BF16)
-        for block in range(2):
-            shift_rows[pl.ds(pl.multiple_of((2 * pair + block) * 8, 8), 8), :] = got[
-                64:72, EDGES * block : EDGES * block + EDGES
-            ]
+        one, none = jnp.ones((), BF16), jnp.zeros((), BF16)
+        for pair in [turn * GATHER + at for at in range(GATHER)]:
+            hits = []
+            for block in range(2):
+                spot = spots[pl.ds(2 * pair + block, 1), :].astype(jnp.int16)
+                hits.append(jnp.where(rows == spot, one, none))
+            got = dot_nn(turned[...], jnp.concatenate(hits, axis=1))
+            scalars[pair] = got[0:64].astype(BF16)
+            for block in range(2):
+                shift_rows[pl.ds(pl.multiple_of((2 * pair + block) * 8, 8), 8), :] = got[
+                    64:72, EDGES * block : EDGES * block + EDGES
+                ]
         return 0
 
-    lax.fori_loop(0, PAIRS, gather, 0)
-
-    slots = lane_slot((BLOCKS, EDGES))
-    centre_rows = over_edges([centres[:, j : j + 1] for j in range(4)], slots)
+    lax.fori_loop(0, PAIRS // GATHER, gather, 0)
+    if stop == 1:
+        return
+
     vector = []
-    for axis, (one, other) in enumerate(zip(coordinates(neighbours), coordinates(centre_rows))):
+    for axis in range(3):
         near = shift_rows[pl.ds(axis, BLOCKS, stride=8), :]
         far = over_edges([centre_shift[j][axis] for j in range(4)], slots)
-        vector.append((one - other).astype(F32) * site_spacing + (near - far))
+        vector.append(steps[axis] + (near - far))
     distance = jnp.sqrt(vector[0] * vector[0] + vector[1] * vector[1] + vector[2] * vector[2])
     inverse = 1.0 / distance
     ux, uy, uz = [part * inverse for part in vector]
@@ -333,31 +481,10 @@
     for m in range(8):
         sphere_rows[pl.ds(m, BLOCKS, stride=8), :] = sphere[m]
 
-    mask = slot_mask()
-    mask_b = mask.astype(BF16)
-    w_pair = w_pair_ref[...]
-    centre_part = dot_nn(
-        centre_slim[:, 0:64].astype(BF16), w_pair[0:64]
-    )
-    centre_slim[...] = centre_part
-    radial = w_radial_ref[...]
-    radial_high, radial_low = split(radial)
-    radial_rows = jnp.concatenate([radial_high.astype(F32), radial_low.astype(F32)], axis=0).astype(BF16)
-    w_mix = w_mix_ref[...].astype(F32)
-    mix_turned = w_mix.T
-    mix_turned = jnp.concatenate(
-        [mix_turned[128:192], mix_turned[64:128], mix_turned[0:64]], axis=0
-    )
-    mix_back = mix_turned.T.astype(BF16)
-    mix_turned = mix_turned.astype(BF16)
-    update = jnp.concatenate([w_self_ref[...], w_tensor_ref[...]], axis=0)
-    update_turned = update.astype(F32).T.astype(BF16)
-    w_out = jnp.broadcast_to(w_out_ref[...].astype(F32), (128, 128)).T
-    w_out = jnp.concatenate([w_out, w_out], axis=1)
-    low_half = lax.broadcasted_iota(jnp.int32, (8, 128), 1) < 64
-    nothing = jnp.zeros((8, 128), F32)
-
-    group = 4
+    centre_slim[...] = dot_nn(centre_slim[:, 0:64].astype(BF16), w_pair[0:64])
+
+    if stop == 2:
+        return
 
     def latents(pair):
         at = pl.multiple_of(8 * pair, 8)
@@ -413,21 +540,45 @@
         value = x * gate
         return value, gate + value * (1.0 - gate)
 
-    def one_group(turn, _):
-        pairs = [turn * group + g for g in range(group)]
-        each = range(group)
-        x1 = [latents(p) for p in pairs]
+    each = range(FIRST)
+
+    def first_group(turn, _):
+        pairs = [turn * FIRST + g for g in each]
+        first = [silu_parts(latents(p)) for p in pairs]
+        for g in each:
+            latent = first[g][0].astype(BF16)
+            latent_rows[pairs[g]] = latent
+            slope_rows[pairs[g]] = first[g][1]
+            mixing_rows[pairs[g]] = dot_nn(mix_turned, latent)
+        return 0
+
+    lax.fori_loop(0, PAIRS // FIRST, first_group, 0)
+    if stop == 3:
+        return
+
+    wide_ready()
+    for place in range(4):
+        hits = jnp.where(centre_spots[:, place : place + 1] == lanes_of_rows, 1.0, 0.0).astype(BF16)
+        got = dot_nn(hits, wide[...])
+        for at in range(WIDE // 128):
+            centre_wide[at, pl.ds(place, BLOCKS, stride=4), :] = got[:, 128 * at : 128 * at + 128]
+
+    if stop == 4:
+        return
+
+    def second_group(turn, _):
+        each = range(SECOND)
+        pairs = [turn * SECOND + g for g in each]
         sides = [tensors(p) for p in pairs]
         contracted = [dot_nn(sides[g][0], spheres(pairs[g])) for g in each]
-        first = [silu_parts(x) for x in x1]
-        latent = [value.astype(BF16) for value, _ in first]
-        mixing = [dot_nn(mix_turned, value) for value in latent]
+        mixing = [mixing_rows[p] for p in pairs]
         coupled = []
         for g in each:
             product = mixing[g] * contracted[g]
             coupled.append((product[0:64] + product[64:128] + product[128:192]).astype(BF16))
         hidden_in = [
-            dot_nn(update_turned, jnp.concatenate([latent[g], coupled[g]], axis=0)) for g in each
+            dot_nn(update_turned, jnp.concatenate([latent_rows[pairs[g]], coupled[g]], axis=0))
+            for g in each
         ]
         second = [silu_parts(x) for x in hidden_in]
         readout = [jnp.sum(value * w_out, axis=0, keepdims=True) for value, _ in second]
@@ -440,7 +591,7 @@
             to_latent = back[g][0:128] + dot_nn(mix_back, to_mixing)
             to_sphere = dot_nn(sides[g][1], to_contracted)
             to_sphere = jnp.sum(to_sphere.reshape(8, 8, LANES) * mask[None], axis=1)
-            to_input = (to_latent * first[g][1]).astype(BF16)
+            to_input = (to_latent * slope_rows[pairs[g]]).astype(BF16)
             to_basis = dot_nn(radial_rows, to_input)
             to_basis = to_basis[0:8] + to_basis[8:16]
             for block in range(2):
@@ -453,7 +604,9 @@
                 )
         return 0
 
-    lax.fori_loop(0, PAIRS // group, one_group, 0)
+    lax.fori_loop(0, PAIRS // SECOND, second_group, 0)
+    if stop == 5:
+        return
 
     def backs(row):
         return back_rows[pl.ds(row, BLOCKS, stride=24), :]
@@ -479,31 +632,35 @@
         jnp.where(active, radial_pull * u + turn_norm * g, 0.0)
         for u, g in ((ux, gx), (uy, gy), (uz, gz))
     ]
-    pulled[...] = jnp.zeros_like(pulled)
     for at, value in enumerate(pulls + [energy]):
         high, low = split(value)
-        low_low = value - high.astype(F32) - low.astype(F32)
-        for part, piece in enumerate((high.astype(F32), low.astype(F32), low_low)):
-            pulled[pl.ds(4 * part + at, BLOCKS, stride=16), :] = piece
-    near_atom = inner_atom(neighbours)
-    far_atom = inner_atom(centre_rows)
-    spots[...] = near_atom
-    shift_rows[0:BLOCKS, :] = far_atom.astype(F32)
-
-    def scatter(block, totals):
-        atoms = lax.broadcasted_iota(jnp.int32, (64, EDGES), 0)
-        near = jnp.where(atoms == spots[pl.ds(block, 1), :], 1.0, 0.0)
-        far = jnp.where(atoms == shift_rows[pl.ds(block, 1), :].astype(jnp.int32), 1.0, 0.0)
-        values = pulled[pl.ds(pl.multiple_of(16 * block, 16), 16), :].astype(BF16)
-        return (
-            totals[0] + dot_nt(values, (far - near).astype(BF16)),
-            totals[1] + dot_nt(values, far.astype(BF16)),
-        )
-
-    start = jnp.zeros((16, 64), F32)
-    force, energy = lax.fori_loop(0, BLOCKS, scatter, (start, start))
-    forces_ref[...] = force[0:3] + force[4:7] + force[8:11]
-    energies_ref[...] = energy[3:4] + energy[7:8] + energy[11:12]
+        pulled[pl.ds(at, BLOCKS, stride=8), :] = high.astype(F32)
+        pulled[pl.ds(4 + at, BLOCKS, stride=8), :] = low.astype(F32)
+    spots[...] = inner_atom(neighbours)
+    far_spots[...] = inner_atom(centre_rows)
+    if stop == 6:
+        return
+
+    def scatter(turn, total):
+        near, far, values = [], [], []
+        atoms = lax.broadcasted_iota(jnp.int32, (64, EDGES), 0).astype(jnp.int16)
+        one, none = jnp.ones((), BF16), jnp.zeros((), BF16)
+        for at in range(SCATTER):
+            block = turn * SCATTER + at
+            spot = spots[pl.ds(block, 1), :].astype(jnp.int16)
+            near.append(jnp.where(atoms == spot, one, none))
+            spot = far_spots[pl.ds(block, 1), :].astype(jnp.int16)
+            far.append(jnp.where(atoms == spot, one, none))
+            values.append(pulled[pl.ds(pl.multiple_of(8 * block, 8), 8), :])
+        near = jnp.concatenate(near, axis=1)
+        far = jnp.concatenate(far, axis=1)
+        values = jnp.concatenate(values, axis=1).astype(BF16)
+        return total + dot_nt(jnp.concatenate([far - near, far], axis=0), values)
+
+    total = lax.fori_loop(0, BLOCKS // SCATTER, scatter, jnp.zeros((128, 8), F32))
+    total = jnp.concatenate([total, jnp.zeros((128, 120), F32)], axis=1).T
+    forces_ref[...] = total[0:3, 0:64] + total[4:7, 0:64]
+    energies_ref[...] = total[3:4, 64:128] + total[7:8, 64:128]
 
 
 def edge_scratch():
@@ -517,56 +674,86 @@
         pltpu.VMEM((8 * BLOCKS, EDGES), F32),
         pltpu.VMEM((8 * BLOCKS, EDGES), F32),
         pltpu.VMEM((24 * BLOCKS, EDGES), F32),
-        pltpu.VMEM((16 * BLOCKS, EDGES), F32),
+        pltpu.VMEM((8 * BLOCKS, EDGES), F32),
+        pltpu.VMEM((BLOCKS, EDGES), jnp.int32),
+        pltpu.VMEM((PAIRS, 128, LANES), BF16),
+        pltpu.VMEM((PAIRS, 128, LANES), F32),
+        pltpu.VMEM((PAIRS, 192, LANES), F32),
     ]
 
 
+HALO_SCRATCH = 13
+
+
+def whole_kernel(features_ref, shifts_ref, *refs):
+    operands, refs = refs[:11], refs[11:]
+    slim, wide, by_slim_out, by_wide_out, by_slim_in, by_wide_in = refs[:6]
+    corner_slim, corner_wide, packed, by_send, by_recv, send_sem, recv_sem = refs[6:HALO_SCRATCH]
+    partners = greet()
+    place_own(features_ref, shifts_ref, slim, wide, by_slim_out, by_wide_out, packed)
+    exchanges = [
+        Exchange(
+            table, out, landed, corner, by_send.at[t], by_recv.at[t], send_sem.at[t], recv_sem.at[t]
+        )
+        for t, (table, out, landed, corner) in enumerate(
+            (
+                (slim, by_slim_out, by_slim_in, corner_slim),
+                (wide, by_wide_out, by_wide_in, corner_wide),
+            )
+        )
+    ]
+
+    def slim_ready():
+        meet(partners)
+        for exchange in exchanges:
+            exchange.start_far()
+        for exchange in exchanges:
+            exchange.start_own()
+        for exchange in exchanges:
+            exchange.pass_on()
+        exchanges[0].arrive()
+
+    def wide_ready():
+        exchanges[1].arrive()
+
+    edge_work(None, slim_ready, wide_ready, slim, wide, *operands, *refs[HALO_SCRATCH:])
+    for exchange in exchanges:
+        exchange.close()
+
+
 VMEM = pl.BlockSpec(memory_space=pltpu.VMEM)
 
 
-def halo(features, shifts):
+def whole(*operands):
     return pl.pallas_call(
-        halo_kernel,
-        out_shape=(
-            jax.ShapeDtypeStruct((ROWS, SLIM), BF16),
-            jax.ShapeDtypeStruct((ROWS, WIDE), BF16),
-        ),
-        in_specs=[VMEM, VMEM],
-        out_specs=(VMEM, VMEM),
-        scratch_shapes=[
-            pltpu.VMEM((2, 32, SLIM), BF16),
-            pltpu.VMEM((2, 32, WIDE), BF16),
-            pltpu.VMEM((2, 32, SLIM), BF16),
-            pltpu.VMEM((2, 32, WIDE), BF16),
-            pltpu.VMEM((64, SLIM), F32),
-            pltpu.SemaphoreType.DMA((2, 2)),
-            pltpu.SemaphoreType.DMA((2, 2)),
-            pltpu.SemaphoreType.DMA((2, 2, SENDS)),
-            pltpu.SemaphoreType.DMA((2, 2, SENDS)),
-        ],
-        compiler_params=pltpu.CompilerParams(
-            collective_id=0, has_side_effects=True, vmem_limit_bytes=32 * 2**20
-        ),
-        name="halo",
-    )(features, shifts)
-
-
-def edges(slim, wide, *rest):
-    def kernel(*refs):
-        edges_kernel(*refs[:13], refs[13:])
-
-    return pl.pallas_call(
-        kernel,
+        whole_kernel,
         out_shape=(
             jax.ShapeDtypeStruct((1, 64), F32),
             jax.ShapeDtypeStruct((3, 64), F32),
         ),
         in_specs=[VMEM] * 11,
         out_specs=(VMEM, VMEM),
-        scratch_shapes=edge_scratch(),
-        compiler_params=pltpu.CompilerParams(vmem_limit_bytes=48 * 2**20),
-        name="edges",
-    )(slim, wide, *rest)
+        scratch_shapes=[
+            pltpu.VMEM((ROWS, SLIM), BF16),
+            pltpu.VMEM((ROWS, WIDE), BF16),
+            pltpu.VMEM((2, 32, SLIM), BF16),
+            pltpu.VMEM((2, 32, WIDE), BF16),
+            pltpu.VMEM((2, 32, SLIM), BF16),
+            pltpu.VMEM((2, 32, WIDE), BF16),
+            pltpu.VMEM((2, 16, SLIM), BF16),
+            pltpu.VMEM((2, 16, WIDE), BF16),
+            pltpu.VMEM((64, SLIM), F32),
+            pltpu.SemaphoreType.DMA((2, 4)),
+            pltpu.SemaphoreType.DMA((2, 4)),
+            pltpu.SemaphoreType.DMA((2, 3, SENDS)),
+            pltpu.SemaphoreType.DMA((2, 3, SENDS)),
+        ]
+        + edge_scratch(),
+        compiler_params=pltpu.CompilerParams(
+            collective_id=0, has_side_effects=True, vmem_limit_bytes=56 * 2**20
+        ),
+        name="boxes",
+    )(*operands)
 
 
 def per_device(
@@ -582,10 +769,9 @@
     w_tensor,
     w_out,
 ):
-    slim, wide = halo(features.reshape(64, WIDE), shifts.reshape(64, 3))
-    energies, forces = edges(
-        slim,
-        wide,
+    energies, forces = whole(
+        features.reshape(64, WIDE),
+        shifts.reshape(64, 3),
         block_counts.reshape(1, 1),
         block_centres.reshape(BLOCKS, 4),
         block_neighbours.reshape(BLOCKS, EDGES),

time: 88.3 us -> 70.7 us (0.80)
  Pallas kernels: 83 us -> 63.8 us
  local copies, waits for them, and re-layouts: 3.58 us -> 5.3 us
    pallas_call x2 -> x1, Pallas kernels: 83 us -> 63.8 us  [whole(): pl.pallas_call(whole_kernel, out_shape=(jax.ShapeDtypeStruct((1, 64), F32...]
    unnamed x22 -> x11, local copies, waits for them, and re-layouts: 3.58 us -> 5.3 us
where the time goes in v1:
time: 70.7 us; the launch traced here: 70.4 us
  Pallas kernels  63.8 us (90%)
  local copies, waits for them, and re-layouts  5.3 us (7%)
  between operations  1.31 us (2%)
    pallas_call x1, Pallas kernels, whole(): pl.pallas_call(whole_kernel, out_shape=(jax.ShapeDtypeStruct((1, 64), F32...  63.8 us
    unnamed x11, local copies, waits for them, and re-layouts  5.3 us

profile of v1, /device:TPU:1, one launch (start us, length us, event | category | flops | bytes accessed | tf_op | source)
XLA Modules:
  0.0 70.4 jit_solution(15834730292216221459)
XLA Ops:
  0.6 0.0 copy-start
  1.3 1.4 %copy.13 = bf16[1,1,1,64,3]{4,3,2,1,0:T(8,128)(2,1)} copy(bf16[1,1,1,64,3]{3,4,2,1,0:T(4,128)(2,1)} %param.12) | data formatting | bytes 768 | tf_op args[1]
  2.7 1.4 %copy.14 = s32[1,1,1,48,4]{4,3,2,1,0:T(8,128)} copy(s32[1,1,1,48,4]{3,4,2,1,0:T(4,128)} %param.14) | data formatting | bytes 1536 | tf_op args[3]
  4.0 0.0 copy-done
  4.0 0.7 %copy.15.refs_5_ = bf16[128,192]{1,0:T(8,128)(2,1)} copy(bf16[128,192]{0,1:T(8,128)(2,1)S(1)} %copy-done) | data formatting | bytes 98304 | tf_op args[7]
  4.8 63.8 %boxes.1 = (f32[1,64]{1,0:T(1,128)}, f32[3,64]{1,0:T(4,128)}) custom-call(bf16[64,640]{1,0:T(8,128)(2,1)} %bitcast.10, bf16[64,3]{1,0:T(8,128)(2,1)} %bitcast.11, s32[1,1]{1,0:T(1,128)} %bitcast.8.refs_0_, s32[48,4]{1,0:T(8,128)} %bitcast.9, s32[48,128]{1,0:T(8,128)} %bitcast.12, bf16[128,128]{1,0:T(8,128)(2,1)} %refs_3_.1, f32[8,128]{1,0:T(8,128)} %refs_4_.1, ...), custom_call_target="tpu_custom_call" | custom-call | tf_op jit(solution)/shard_map/boxes/pallas_call | solution.py:728
  68.6 0.0 copy-start.1
  68.6 0.7 copy-done.1
  69.3 0.0 copy-start.2
  69.3 0.6 copy.16
  69.8 0.1 copy-done.2
  69.9 0.5 copy.19
Async XLA Ops:
  0.6 3.4 %copy-start = (bf16[128,192]{0,1:T(8,128)(2,1)S(1)}, bf16[128,192]{0,1:T(8,128)(2,1)}, u32[]{:S(2)}) copy-start(bf16[128,192]{0,1:T(8,128)(2,1)} %param.18) | copy-start | bytes 147460
  68.6 0.7 copy-start.1
  69.3 0.7 copy-start.2

commit v2 on v1

--- a/solution.py
+++ b/solution.py
@@ -1,3 +1,4 @@
+import functools
 import math
 
 import jax
@@ -65,7 +66,7 @@
 def place_own(features_ref, shifts_ref, slim, wide, by_slim_out, by_wide_out, packed):
     packed[...] = jnp.zeros_like(packed)
     packed[:, 0:64] = features_ref[:, 0:64].astype(F32)
-    packed[:, 64:67] = shifts_ref[...].astype(F32)
+    packed[:, 64:72] = turned_rows(shifts_ref[...].astype(F32))[0:64]
     own = [4 * ox + 2 * oy + oz for oz in range(2) for ox in range(2) for oy in range(2)]
     for source, table, out in (
         (packed[...], slim, by_slim_out),
@@ -85,42 +86,107 @@
     table[first : first + 16 * count, :] = jnp.concatenate(pieces, axis=0).astype(BF16)
 
 
-def low_wrap():
-    return lax.axis_index("bz") == 0
-
-
-def high_wrap():
-    return lax.axis_index("bz") == lax.axis_size("bz") - 1
-
-
-def greet():
+class Place:
+    def __init__(self):
+        self.bx, self.by, self.bz = (lax.axis_index(axis) for axis in ("bx", "by", "bz"))
+        self.ends = lax.axis_size("bz") - 1
+        self.x, self.z_hi = lax.rem(self.by, 4), lax.div(self.by, 4)
+        self.first_x, self.last_x = self.x == 0, self.x == 3
+        self.edge = self.first_x | self.last_x
+        self.early = self.z_hi == 0
+        self.late = self.z_hi == 1
+        self.low = self.bz == 0
+        self.high = self.bz == self.ends
+        self.middle = lax.div(lax.axis_size("bz"), 2)
+        self.upper = self.bz >= self.middle
+        self.by_helper = jnp.logical_not(self.edge) & self.late & (self.bz < self.middle)
+        self.wrap_helper = self.late & (self.bz == self.middle)
+
+
+def flips(place, side):
+    return place.last_x if side == 0 else place.first_x
+
+
+def signal(semaphore, device):
+    pl.semaphore_signal(semaphore, inc=1, device_id=device, device_id_type=MESH)
+
+
+def as_count(condition, amount):
+    return jnp.where(condition, amount, 0)
+
+
+def greet(place):
     barrier = pltpu.get_barrier_semaphore()
-    partners = [(0, 1, 0), (0, -1, 0)] + [
-        (dx, 0, dz) for dx in (-1, 0, 1) for dz in (-1, 0, 1) if dx or dz
-    ]
-
-    def signal(dx, dy, dz):
-        pl.semaphore_signal(barrier, inc=1, device_id=at_device(dx, dy, dz), device_id_type=MESH)
-
-    for wraps, dz in ((low_wrap, -1), (high_wrap, 1)):
-
-        @pl.when(wraps())
+    for dx in (-1, 1):
+        signal(barrier, at_device(dx, 0, 0))
+    for side, dy in ((0, 1), (1, -1)):
+
+        @pl.when(jnp.logical_not(flips(place, side)) | place.early)
         def _():
-            signal(0, 1, dz)
-            signal(0, -1, dz)
-
-    for partner in partners:
-        signal(*partner)
-    return len(partners)
-
-
-def meet(count):
-    ends = jnp.where(low_wrap() | high_wrap(), 2, 0)
-    pl.semaphore_wait(pltpu.get_barrier_semaphore(), count + ends)
+            signal(barrier, at_device(0, dy, 0))
+
+    for dx in (-1, 0, 1):
+        signal(barrier, at_device(dx, 0, -1))
+
+        @pl.when(jnp.logical_not(place.high))
+        def _():
+            signal(barrier, at_device(dx, 0, 1))
+
+    for side, dy in ((0, 1), (1, -1)):
+
+        @pl.when(place.low)
+        def _():
+            signal(barrier, at_device(0, dy, -1))
+
+        @pl.when(place.high & place.early & flips(place, side))
+        def _():
+            signal(barrier, at_device(0, dy, 1))
+
+    @pl.when(place.edge & place.upper)
+    def _():
+        near_first = place.first_x == place.early
+        signal(barrier, (place.bx, jnp.where(near_first, 5, 6), place.bz - place.middle))
+
+    @pl.when(place.late & place.low)
+    def _():
+        signal(barrier, (place.bx, place.by, place.middle))
+
+    @pl.when(place.late & place.high)
+    def _():
+        for dx in (-1, 0, 1):
+            signal(barrier, (wrapped("bx", dx), place.by, place.middle))
+
+        for side, dy in ((0, 1), (1, -1)):
+
+            @pl.when(jnp.logical_not(flips(place, side)))
+            def _():
+                signal(barrier, (place.bx, place.by + dy, place.middle))
+
+
+def meet(place):
+    count = 2 + as_count(jnp.logical_not(place.edge), 1) + 1
+    count = count + as_count(place.edge & place.late, 1)
+    count = count + as_count(jnp.logical_not(place.low), 3) + 3
+    count = count + as_count(place.high, 2)
+    count = count + as_count(place.low & place.late & place.edge, 1)
+    count = count + as_count(place.by_helper, 2)
+    count = count + as_count(place.wrap_helper, 5 + as_count(jnp.logical_not(place.edge), 1))
+    pl.semaphore_wait(pltpu.get_barrier_semaphore(), count)
+
+
+def help_others(place, go):
+    @pl.when(place.by_helper)
+    def _():
+        signal(go.at[0], (place.bx, jnp.where(place.x == 1, 0, 3), place.bz + place.middle))
+
+    @pl.when(place.wrap_helper)
+    def _():
+        signal(go.at[1], (place.bx, place.by, 0))
 
 
 class Exchange:
-    def __init__(self, table, out, landed, corner, by_send, by_recv, send, recv):
+    def __init__(self, place, table, out, landed, corner, by_send, by_recv, send, recv):
+        self.place = place
         self.table, self.out, self.landed, self.corner = table, out, landed, corner
         self.by_send, self.by_recv, self.send, self.recv = by_send, by_recv, send, recv
 
@@ -134,39 +200,33 @@
             device_id_type=MESH,
         )
 
-    def by_copies(self):
-        return [
-            self.copy(
-                self.out.at[1 - side],
-                self.landed.at[side],
-                self.by_send.at[side],
-                self.by_recv.at[side],
-                0,
-                1 - 2 * side,
-                0,
-            )
-            for side in range(2)
-        ]
-
-    def corner_copies(self, dz):
-        source = 16 if dz > 0 else 0
-        return [
-            self.copy(
-                self.out.at[1 - side, pl.ds(source, 16)],
-                self.corner.at[side],
-                self.by_send.at[2 + side],
-                self.by_recv.at[2 + side],
-                0,
-                1 - 2 * side,
-                dz,
-            )
-            for side in range(2)
-        ]
+    def by_copy(self, side):
+        return self.copy(
+            self.out.at[1 - side],
+            self.landed.at[side],
+            self.by_send.at[side],
+            self.by_recv.at[side],
+            0,
+            1 - 2 * side,
+            0,
+        )
+
+    def corner_copy(self, dz, side):
+        return self.copy(
+            self.out.at[1 - side, pl.ds(16 if dz > 0 else 0, 16)],
+            self.corner.at[side],
+            self.by_send.at[2 + side],
+            self.by_recv.at[2 + side],
+            0,
+            1 - 2 * side,
+            dz,
+        )
 
     def half_copies(self, half):
         return [
             (
-                self.copy(
+                functools.partial(
+                    self.copy,
                     self.table.at[pl.ds(HALF * half + source, rows)],
                     self.table.at[pl.ds(HALF * half + target, rows)],
                     self.send.at[half, at],
@@ -203,82 +263,207 @@
             ),
         ]
 
-    def start_far(self):
-        for copy in self.by_copies():
-            copy.start()
-        for wraps, dz in ((low_wrap, -1), (high_wrap, 1)):
-
-            @pl.when(wraps())
+    def start_by(self, far):
+        for side in range(2):
+
+            @pl.when(flips(self.place, side) if far else jnp.logical_not(flips(self.place, side)))
             def _():
-                for copy in self.corner_copies(dz):
-                    copy.start()
+                self.by_copy(side).start()
+
+    def start_wrap(self, dz):
+        for copy, along in self.half_copies(0):
+            if along == dz:
+                copy().start()
+
+    def start_corners(self, dz, flipped=(True, False)):
+        for side in range(2):
+            if len(flipped) == 2:
+                self.corner_copy(dz, side).start()
+            else:
+
+                @pl.when(flips(self.place, side) == flipped[0])
+                def _():
+                    self.corner_copy(dz, side).start()
 
     def start_own(self):
-        for copy, _ in self.half_copies(0):
-            copy.start()
-
-    def pass_on(self):
-        for copy in self.by_copies():
-            copy.wait_recv()
+        for copy, dz in self.half_copies(0):
+            if dz == 0:
+                copy().start()
+            else:
+
+                @pl.when(jnp.logical_not(self.place.high if dz > 0 else self.place.low))
+                def _():
+                    copy().start()
+
+    def spread_by(self):
         place_octants(self.table, HALF, self.landed, 4)
         for copy, dz in self.half_copies(1):
             if dz == 0:
-                copy.start()
+                copy().start()
             else:
 
-                @pl.when(jnp.logical_not(high_wrap() if dz > 0 else low_wrap()))
+                @pl.when(jnp.logical_not(self.place.high if dz > 0 else self.place.low))
                 def _():
-                    copy.start()
-
-        for wraps, dz in ((low_wrap, -1), (high_wrap, 1)):
-
-            @pl.when(wraps())
-            def _():
-                for copy in self.corner_copies(dz):
-                    copy.wait_recv()
-                place_octants(self.table, HALF + (64 if dz < 0 else 96), self.corner, 2)
-                for copy in self.late_copies(int(dz > 0)):
-                    copy.start()
+                    copy().start()
+
+    def wait_corners(self, dz):
+        for side in range(2):
+            self.corner_copy(dz, side).wait_recv()
+
+    def take_corners(self, dz):
+        place_octants(self.table, HALF + (64 if dz < 0 else 96), self.corner, 2)
+        for copy in self.late_copies(int(dz > 0)):
+            copy.start()
+
+    def wait_wrap(self, dz):
+        for copy, along in self.half_copies(0):
+            if along == dz:
+                copy().wait_recv()
 
     def arrive(self):
-        for copy, _ in self.half_copies(0):
-            copy.wait_recv()
+        for copy, dz in self.half_copies(0):
+            if self.wraps_waited(dz):
+
+                @pl.when(jnp.logical_not(self.place.low & self.place.early))
+                def _():
+                    copy().wait_recv()
+            else:
+                copy().wait_recv()
         for copy, dz in self.half_copies(1):
             if dz == 0:
-                copy.wait_recv()
+                copy().wait_recv()
             else:
 
-                @pl.when(jnp.logical_not(low_wrap() if dz > 0 else high_wrap()))
+                @pl.when(jnp.logical_not(self.place.low if dz > 0 else self.place.high))
                 def _():
-                    copy.wait_recv()
-
-        for wraps, high in ((low_wrap, 0), (high_wrap, 1)):
-
-            @pl.when(wraps())
+                    copy().wait_recv()
+
+        for wraps, high in ((self.place.low, 0), (self.place.high, 1)):
+
+            @pl.when(wraps)
             def _():
                 for copy in self.late_copies(high):
                     copy.wait_recv()
 
+    def wraps_waited(self, dz):
+        return False
+
     def close(self):
-        for copy in self.by_copies():
-            copy.wait_send()
+        for side in range(2):
+            self.by_copy(side).wait_send()
         for copy, _ in self.half_copies(0):
-            copy.wait_send()
+            copy().wait_send()
         for copy, dz in self.half_copies(1):
             if dz == 0:
-                copy.wait_send()
+                copy().wait_send()
             else:
 
-                @pl.when(jnp.logical_not(high_wrap() if dz > 0 else low_wrap()))
+                @pl.when(jnp.logical_not(self.place.high if dz > 0 else self.place.low))
                 def _():
+                    copy().wait_send()
+
+        for wraps, high in ((self.place.low, 0), (self.place.high, 1)):
+
+            @pl.when(wraps)
+            def _():
+                for side in range(2):
+                    self.corner_copy(2 * high - 1, side).wait_send()
+                for copy in self.late_copies(high):
                     copy.wait_send()
 
-        for wraps, high in ((low_wrap, 0), (high_wrap, 1)):
-
-            @pl.when(wraps())
-            def _():
-                for copy in self.corner_copies(2 * high - 1) + self.late_copies(high):
-                    copy.wait_send()
+
+class SlimExchange(Exchange):
+    def wraps_waited(self, dz):
+        return dz > 0
+
+
+def start_first(place, exchanges):
+    slim, wide = exchanges
+
+    @pl.when(place.edge & place.late)
+    def _():
+        for exchange in exchanges:
+            exchange.start_by(True)
+
+    @pl.when(place.high)
+    def _():
+        slim.start_corners(1)
+        slim.start_wrap(1)
+        wide.start_corners(1)
+
+    @pl.when(place.low & place.late)
+    def _():
+        for exchange in exchanges:
+            exchange.start_corners(-1, (True,))
+
+    for exchange in exchanges:
+        exchange.start_by(False)
+    slim.start_own()
+
+
+def start_second(place, exchanges, go):
+    wide = exchanges[1]
+    wide.start_own()
+
+    @pl.when(place.high)
+    def _():
+        wide.start_wrap(1)
+
+    @pl.when(place.edge & place.early & place.upper)
+    def _():
+        pl.semaphore_wait(go.at[0], 1)
+        for exchange in exchanges:
+            exchange.start_by(True)
+
+    @pl.when(place.low & place.late)
+    def _():
+        pl.semaphore_wait(go.at[1], 1)
+        for exchange in exchanges:
+            exchange.start_wrap(-1)
+            exchange.start_corners(-1, (False,))
+
+
+def pass_on(place, exchanges):
+    slim, wide = exchanges
+    for side in range(2):
+        slim.by_copy(side).wait_recv()
+
+    slim.spread_by()
+
+    @pl.when(place.edge & place.early & jnp.logical_not(place.upper))
+    def _():
+        for exchange in exchanges:
+            exchange.start_by(True)
+
+    @pl.when(place.low & place.early)
+    def _():
+        slim.wait_wrap(1)
+        for exchange in exchanges:
+            exchange.start_wrap(-1)
+        slim.wait_corners(-1)
+        for exchange in exchanges:
+            exchange.start_corners(-1)
+        slim.take_corners(-1)
+
+    @pl.when(place.low & place.late)
+    def _():
+        slim.wait_corners(-1)
+        slim.take_corners(-1)
+
+    @pl.when(place.high)
+    def _():
+        slim.wait_corners(1)
+        slim.take_corners(1)
+
+    for side in range(2):
+        wide.by_copy(side).wait_recv()
+    wide.spread_by()
+    for wraps, dz in ((place.low, -1), (place.high, 1)):
+
+        @pl.when(wraps)
+        def _():
+            wide.wait_corners(dz)
+            wide.take_corners(dz)
 
 
 def dot_nn(left, right):
@@ -341,6 +526,12 @@
     return jnp.where(slots < 2, low, high)
 
 
+def turned_rows(value):
+    rows, columns = value.shape
+    value = jnp.concatenate([value, jnp.zeros((8 - rows, columns), F32)], axis=0)
+    return jnp.concatenate([value, jnp.zeros((8, 128 - columns), F32)], axis=1).T
+
+
 def slot_mask():
     slots = lane_slot((8, LANES))
     return jnp.where(slots == lax.broadcasted_iota(jnp.int32, (8, LANES), 0), 1.0, 0.0).astype(F32)
@@ -348,6 +539,7 @@
 
 def edge_work(
     stop,
+    begin,
     slim_ready,
     wide_ready,
     slim,
@@ -378,8 +570,10 @@
     slope_rows,
     mixing_rows,
 ):
+    begin()
+
     neighbours = neighbours_ref[...]
-    centres = centres_ref[...]
+    centres = turned_rows(centres_ref[...].astype(F32))[0:BLOCKS].astype(jnp.int32)
     spots[...] = table_row(neighbours)
     centre_spots = table_row(centres)
     slots = lane_slot((BLOCKS, EDGES))
@@ -393,8 +587,7 @@
     radial = w_radial_ref[...]
     radial_high, radial_low = split(radial)
     radial_rows = jnp.concatenate([radial_high.astype(F32), radial_low.astype(F32)], axis=0).astype(BF16)
-    w_mix = w_mix_ref[...].astype(F32)
-    mix_turned = w_mix.T
+    mix_turned = w_mix_ref[...].astype(F32)
     mix_turned = jnp.concatenate(
         [mix_turned[128:192], mix_turned[64:128], mix_turned[0:64]], axis=0
     )
@@ -659,7 +852,8 @@
 
     total = lax.fori_loop(0, BLOCKS // SCATTER, scatter, jnp.zeros((128, 8), F32))
     total = jnp.concatenate([total, jnp.zeros((128, 120), F32)], axis=1).T
-    forces_ref[...] = total[0:3, 0:64] + total[4:7, 0:64]
+    for axis in range(3):
+        forces_ref[axis] = total[axis : axis + 1, 0:64] + total[4 + axis : 5 + axis, 0:64]
     energies_ref[...] = total[3:4, 64:128] + total[7:8, 64:128]
 
 
@@ -682,41 +876,51 @@
     ]
 
 
-HALO_SCRATCH = 13
+HALO_SCRATCH = 14
 
 
 def whole_kernel(features_ref, shifts_ref, *refs):
     operands, refs = refs[:11], refs[11:]
     slim, wide, by_slim_out, by_wide_out, by_slim_in, by_wide_in = refs[:6]
-    corner_slim, corner_wide, packed, by_send, by_recv, send_sem, recv_sem = refs[6:HALO_SCRATCH]
-    partners = greet()
+    corner_slim, corner_wide, packed = refs[6:9]
+    by_send, by_recv, send_sem, recv_sem, go = refs[9:HALO_SCRATCH]
+    place = Place()
+    greet(place)
     place_own(features_ref, shifts_ref, slim, wide, by_slim_out, by_wide_out, packed)
     exchanges = [
-        Exchange(
-            table, out, landed, corner, by_send.at[t], by_recv.at[t], send_sem.at[t], recv_sem.at[t]
+        kind(
+            place,
+            table,
+            out,
+            landed,
+            corner,
+            by_send.at[t],
+            by_recv.at[t],
+            send_sem.at[t],
+            recv_sem.at[t],
         )
-        for t, (table, out, landed, corner) in enumerate(
+        for t, (kind, table, out, landed, corner) in enumerate(
             (
-                (slim, by_slim_out, by_slim_in, corner_slim),
-                (wide, by_wide_out, by_wide_in, corner_wide),
+                (SlimExchange, slim, by_slim_out, by_slim_in, corner_slim),
+                (Exchange, wide, by_wide_out, by_wide_in, corner_wide),
             )
         )
     ]
 
+    def begin():
+        meet(place)
+        help_others(place, go)
+        start_first(place, exchanges)
+
     def slim_ready():
-        meet(partners)
-        for exchange in exchanges:
-            exchange.start_far()
-        for exchange in exchanges:
-            exchange.start_own()
-        for exchange in exchanges:
-            exchange.pass_on()
+        start_second(place, exchanges, go)
+        pass_on(place, exchanges)
         exchanges[0].arrive()
 
     def wide_ready():
         exchanges[1].arrive()
 
-    edge_work(None, slim_ready, wide_ready, slim, wide, *operands, *refs[HALO_SCRATCH:])
+    edge_work(None, begin, slim_ready, wide_ready, slim, wide, *operands, *refs[HALO_SCRATCH:])
     for exchange in exchanges:
         exchange.close()
 
@@ -729,7 +933,7 @@
         whole_kernel,
         out_shape=(
             jax.ShapeDtypeStruct((1, 64), F32),
-            jax.ShapeDtypeStruct((3, 64), F32),
+            jax.ShapeDtypeStruct((3, 1, 64), F32),
         ),
         in_specs=[VMEM] * 11,
         out_specs=(VMEM, VMEM),
@@ -747,6 +951,7 @@
             pltpu.SemaphoreType.DMA((2, 4)),
             pltpu.SemaphoreType.DMA((2, 3, SENDS)),
             pltpu.SemaphoreType.DMA((2, 3, SENDS)),
+            pltpu.SemaphoreType.REGULAR((2,)),
         ]
         + edge_scratch(),
         compiler_params=pltpu.CompilerParams(
@@ -771,13 +976,13 @@
 ):
     energies, forces = whole(
         features.reshape(64, WIDE),
-        shifts.reshape(64, 3),
+        shifts.reshape(64, 3).T,
         block_counts.reshape(1, 1),
-        block_centres.reshape(BLOCKS, 4),
+        block_centres.reshape(BLOCKS, 4).T,
         block_neighbours.reshape(BLOCKS, EDGES),
         w_pair,
         w_radial,
-        w_mix,
+        w_mix.T,
         w_self,
         w_tensor,
         w_out.reshape(1, 128),

time: 70.7 us -> 66 us (0.934)
  local copies, waits for them, and re-layouts: 5.3 us -> 1.69 us
  Pallas kernels: 63.8 us -> 62.8 us
    unnamed x11 -> x6, local copies, waits for them, and re-layouts: 5.3 us -> 1.69 us
    pallas_call x1, Pallas kernels: 63.8 us -> 62.8 us  [whole(): pl.pallas_call(whole_kernel, out_shape=(jax.ShapeDtypeStruct((1, 64), F32...]
where the time goes in v2:
time: 66 us; the launch traced here: 65.8 us
  Pallas kernels  62.8 us (95%)
  local copies, waits for them, and re-layouts  1.69 us (3%)
  between operations  1.3 us (2%)
    pallas_call x1, Pallas kernels, whole(): pl.pallas_call(whole_kernel, out_shape=(jax.ShapeDtypeStruct((1, 64), F32...  62.8 us
    unnamed x6, local copies, waits for them, and re-layouts  1.69 us

profile of v2, /device:TPU:1, one launch (start us, length us, event | category | flops | bytes accessed | tf_op | source)
XLA Modules:
  0.0 65.8 jit_solution(1772241487748611335)
XLA Ops:
  1.3 62.8 %boxes.1 = (f32[1,64]{1,0:T(1,128)}, f32[3,1,64]{2,1,0:T(1,128)}) custom-call(bf16[64,640]{1,0:T(8,128)(2,1)} %bitcast.16, bf16[3,64]{1,0:T(4,128)(2,1)} %bitcast.21, s32[1,1]{1,0:T(1,128)} %bitcast.15.refs_0_, s32[4,48]{1,0:T(4,128)} %bitcast.19, s32[48,128]{1,0:T(8,128)} %bitcast.18, bf16[128,128]{1,0:T(8,128)(2,1)} %refs_3_.1, f32[8,128]{1,0:T(8,128)} %refs_4_.1, ...), custom_call_target="tpu_custom_call" | custom-call | tf_op jit(solution)/shard_map/boxes/pallas_call | solution.py:932
  64.1 0.0 copy-start.1
  64.1 0.0 copy-start
  64.1 0.6 copy-done.1
  64.7 0.5 copy.17
  65.2 0.0 copy-done
  65.2 0.6 copy.18
Async XLA Ops:
  64.1 0.6 copy-start.1
  64.1 1.1 %copy-start = (f32[3,1,64]{2,1,0:T(1,128)S(1)}, f32[3,1,64]{2,1,0:T(1,128)}, u32[]{:S(2)}) copy-start(f32[3,1,64]{2,1,0:T(1,128)} %get-tuple-element.5) | copy-start | bytes 2308

commit v3 on v2

--- a/solution.py
+++ b/solution.py
@@ -28,7 +28,7 @@
 SCATTER = 24
 GATHER = 12
 FIRST = 12
-SECOND = 8
+SECOND = 12
 LANES = 2 * EDGES
 
 
@@ -430,19 +430,10 @@
 
     slim.spread_by()
 
-    @pl.when(place.edge & place.early & jnp.logical_not(place.upper))
-    def _():
-        for exchange in exchanges:
-            exchange.start_by(True)
-
     @pl.when(place.low & place.early)
     def _():
         slim.wait_wrap(1)
-        for exchange in exchanges:
-            exchange.start_wrap(-1)
         slim.wait_corners(-1)
-        for exchange in exchanges:
-            exchange.start_corners(-1)
         slim.take_corners(-1)
 
     @pl.when(place.low & place.late)
@@ -464,6 +455,17 @@
         def _():
             wide.wait_corners(dz)
             wide.take_corners(dz)
+
+    @pl.when(place.edge & place.early & jnp.logical_not(place.upper))
+    def _():
+        for exchange in exchanges:
+            exchange.start_by(True)
+
+    @pl.when(place.low & place.early)
+    def _():
+        for exchange in exchanges:
+            exchange.start_wrap(-1)
+            exchange.start_corners(-1)
 
 
 def dot_nn(left, right):
@@ -553,8 +555,7 @@
     w_self_ref,
     w_tensor_ref,
     w_out_ref,
-    energies_ref,
-    forces_ref,
+    result_ref,
     turned,
     spots,
     scalars,
@@ -566,7 +567,8 @@
     back_rows,
     pulled,
     far_spots,
-    latent_rows,
+    sphere_spread,
+    self_rows,
     slope_rows,
     mixing_rows,
 ):
@@ -595,6 +597,8 @@
     mix_turned = mix_turned.astype(BF16)
     update = jnp.concatenate([w_self_ref[...], w_tensor_ref[...]], axis=0)
     update_turned = update.astype(F32).T.astype(BF16)
+    from_latent = jnp.concatenate([mix_turned, update_turned[:, 0:128]], axis=0)
+    tensor_turned = update_turned[:, 128:192]
     w_out = jnp.broadcast_to(w_out_ref[...].astype(F32), (128, 128)).T
     w_out = jnp.concatenate([w_out, w_out], axis=1)
     low_half = lax.broadcasted_iota(jnp.int32, (8, 128), 1) < 64
@@ -740,9 +744,11 @@
         first = [silu_parts(latents(p)) for p in pairs]
         for g in each:
             latent = first[g][0].astype(BF16)
-            latent_rows[pairs[g]] = latent
             slope_rows[pairs[g]] = first[g][1]
-            mixing_rows[pairs[g]] = dot_nn(mix_turned, latent)
+            made = dot_nn(from_latent, latent)
+            mixing_rows[pairs[g]] = made[0:192]
+            self_rows[pairs[g]] = made[192:320]
+            sphere_spread[pairs[g]] = spheres(pairs[g])
         return 0
 
     lax.fori_loop(0, PAIRS // FIRST, first_group, 0)
@@ -763,35 +769,38 @@
         each = range(SECOND)
         pairs = [turn * SECOND + g for g in each]
         sides = [tensors(p) for p in pairs]
-        contracted = [dot_nn(sides[g][0], spheres(pairs[g])) for g in each]
+        contracted = [dot_nn(sides[g][0], sphere_spread[pairs[g]]) for g in each]
         mixing = [mixing_rows[p] for p in pairs]
         coupled = []
         for g in each:
             product = mixing[g] * contracted[g]
             coupled.append((product[0:64] + product[64:128] + product[128:192]).astype(BF16))
         hidden_in = [
-            dot_nn(update_turned, jnp.concatenate([latent_rows[pairs[g]], coupled[g]], axis=0))
-            for g in each
+            self_rows[pairs[g]] + dot_nn(tensor_turned, coupled[g]) for g in each
         ]
         second = [silu_parts(x) for x in hidden_in]
         readout = [jnp.sum(value * w_out, axis=0, keepdims=True) for value, _ in second]
         back = [dot_nn(update, (slope * w_out).astype(BF16)) for _, slope in second]
+        to_mixing, to_contracted = [], []
         for g in each:
             cotangent = back[g][128:192].astype(BF16).astype(F32)
             cotangents = jnp.concatenate([cotangent, cotangent, cotangent], axis=0)
-            to_mixing = (cotangents * contracted[g]).astype(BF16)
-            to_contracted = (cotangents[0:128] * mixing[g][0:128]).astype(BF16)
-            to_latent = back[g][0:128] + dot_nn(mix_back, to_mixing)
-            to_sphere = dot_nn(sides[g][1], to_contracted)
-            to_sphere = jnp.sum(to_sphere.reshape(8, 8, LANES) * mask[None], axis=1)
-            to_input = (to_latent * slope_rows[pairs[g]]).astype(BF16)
-            to_basis = dot_nn(radial_rows, to_input)
-            to_basis = to_basis[0:8] + to_basis[8:16]
+            to_mixing.append((cotangents * contracted[g]).astype(BF16))
+            to_contracted.append((cotangents[0:128] * mixing[g][0:128]).astype(BF16))
+        to_latent = [dot_nn(mix_back, to_mixing[g]) for g in each]
+        to_sphere = [dot_nn(sides[g][1], to_contracted[g]) for g in each]
+        to_input = [
+            ((back[g][0:128] + to_latent[g]) * slope_rows[pairs[g]]).astype(BF16) for g in each
+        ]
+        to_basis = [dot_nn(radial_rows, to_input[g]) for g in each]
+        for g in each:
+            sphere = jnp.sum(to_sphere[g].reshape(8, 8, LANES) * mask[None], axis=1)
+            basis = to_basis[g][0:8] + to_basis[g][8:16]
             for block in range(2):
                 at = (2 * pairs[g] + block) * 24
                 lanes = slice(EDGES * block, EDGES * block + EDGES)
-                back_rows[pl.ds(pl.multiple_of(at, 8), 8), :] = to_sphere[:, lanes]
-                back_rows[pl.ds(pl.multiple_of(at + 8, 8), 8), :] = to_basis[:, lanes]
+                back_rows[pl.ds(pl.multiple_of(at, 8), 8), :] = sphere[:, lanes]
+                back_rows[pl.ds(pl.multiple_of(at + 8, 8), 8), :] = basis[:, lanes]
                 back_rows[pl.ds(pl.multiple_of(at + 16, 8), 8), :] = jnp.broadcast_to(
                     readout[g][:, lanes], (8, EDGES)
                 )
@@ -852,9 +861,10 @@
 
     total = lax.fori_loop(0, BLOCKS // SCATTER, scatter, jnp.zeros((128, 8), F32))
     total = jnp.concatenate([total, jnp.zeros((128, 120), F32)], axis=1).T
+    total = total[0:4] + total[4:8]
     for axis in range(3):
-        forces_ref[axis] = total[axis : axis + 1, 0:64] + total[4 + axis : 5 + axis, 0:64]
-    energies_ref[...] = total[3:4, 64:128] + total[7:8, 64:128]
+        result_ref[axis] = total[axis : axis + 1, 0:64]
+    result_ref[3] = total[3:4, 64:128]
 
 
 def edge_scratch():
@@ -870,7 +880,8 @@
         pltpu.VMEM((24 * BLOCKS, EDGES), F32),
         pltpu.VMEM((8 * BLOCKS, EDGES), F32),
         pltpu.VMEM((BLOCKS, EDGES), jnp.int32),
-        pltpu.VMEM((PAIRS, 128, LANES), BF16),
+        pltpu.VMEM((PAIRS, 80, LANES), BF16),
+        pltpu.VMEM((PAIRS, 128, LANES), F32),
         pltpu.VMEM((PAIRS, 128, LANES), F32),
         pltpu.VMEM((PAIRS, 192, LANES), F32),
     ]
@@ -880,7 +891,7 @@
 
 
 def whole_kernel(features_ref, shifts_ref, *refs):
-    operands, refs = refs[:11], refs[11:]
+    operands, refs = refs[:10], refs[10:]
     slim, wide, by_slim_out, by_wide_out, by_slim_in, by_wide_in = refs[:6]
     corner_slim, corner_wide, packed = refs[6:9]
     by_send, by_recv, send_sem, recv_sem, go = refs[9:HALO_SCRATCH]
@@ -931,12 +942,9 @@
 def whole(*operands):
     return pl.pallas_call(
         whole_kernel,
-        out_shape=(
-            jax.ShapeDtypeStruct((1, 64), F32),
-            jax.ShapeDtypeStruct((3, 1, 64), F32),
-        ),
+        out_shape=jax.ShapeDtypeStruct((4, 1, 64), F32),
         in_specs=[VMEM] * 11,
-        out_specs=(VMEM, VMEM),
+        out_specs=VMEM,
         scratch_shapes=[
             pltpu.VMEM((ROWS, SLIM), BF16),
             pltpu.VMEM((ROWS, WIDE), BF16),
@@ -974,7 +982,7 @@
     w_tensor,
     w_out,
 ):
-    energies, forces = whole(
+    result = whole(
         features.reshape(64, WIDE),
         shifts.reshape(64, 3).T,
         block_counts.reshape(1, 1),
@@ -987,7 +995,7 @@
         w_tensor,
         w_out.reshape(1, 128),
     )
-    return energies.reshape(1, 1, 1, 64), forces.reshape(1, 1, 1, 3, 64)
+    return result[3].reshape(1, 1, 1, 64), result[0:3].reshape(1, 1, 1, 3, 64)
 
 
 def solution(mesh):

time: 66 us -> 61.7 us (0.935)
  the two profiles are of different devices: /device:TPU:1 before, /device:TPU:641 now
where the time goes in v3:
time: 61.7 us; the launch traced here: 61.4 us
  Pallas kernels  57.7 us (94%)
  local copies, waits for them, and re-layouts  2.44 us (4%)
  between operations  1.29 us (2%)
    pallas_call x1, Pallas kernels, whole(): pl.pallas_call(whole_kernel, out_shape=jax.ShapeDtypeStruct((4, 1, 64), F...  57.7 us
    unnamed x1, local copies, waits for them, and re-layouts  1.24 us

profile of v3, /device:TPU:641, one launch (start us, length us, event | category | flops | bytes accessed | tf_op | source)
XLA Modules:
  0.0 61.4 jit_solution(5445126863288931213)
XLA Ops:
  1.3 57.7 %boxes.1 = f32[4,1,64]{2,1,0:T(1,128)} custom-call(bf16[64,640]{1,0:T(8,128)(2,1)} %bitcast.18, bf16[3,64]{1,0:T(4,128)(2,1)} %bitcast.22, s32[1,1]{1,0:T(1,128)} %bitcast.17.refs_0_, s32[4,48]{1,0:T(4,128)} %bitcast.21, s32[48,128]{1,0:T(8,128)} %bitcast.20, bf16[128,128]{1,0:T(8,128)(2,1)} %refs_3_.1, f32[8,128]{1,0:T(8,128)} %refs_4_.1, ...), custom_call_target="tpu_custom_call" | custom-call | tf_op jit(solution)/shard_map/boxes/pallas_call | solution.py:943
  59.0 1.2 %slice_bitcast_fusion.1 = f32[1,1,1,64]{3,2,1,0:T(1,128)} fusion(f32[4,1,64]{2,1,0:T(1,128)} %boxes.1), kind=kLoop, calls=%fused_computation.1 | loop fusion | bytes 512 | tf_op jit(solution)/shard_map/reshape;squeeze | solution.py:998
  60.2 1.2 %slice_bitcast_fusion = f32[1,1,1,3,64]{4,2,3,1,0:T(1,128)} fusion(f32[4,1,64]{2,1,0:T(1,128)} %boxes.1), kind=kLoop, calls=%fused_computation | loop fusion | bytes 1536

commit v4 on v3

--- a/solution.py
+++ b/solution.py
@@ -26,8 +26,8 @@
 EDGES = 128
 PAIRS = BLOCKS // 2
 SCATTER = 24
-GATHER = 12
-FIRST = 12
+GATHER = 24
+FIRST = 24
 SECOND = 12
 LANES = 2 * EDGES
 
@@ -429,6 +429,16 @@
         slim.by_copy(side).wait_recv()
 
     slim.spread_by()
+    lower = place.edge & place.early & jnp.logical_not(place.upper)
+    hurried = place.bz >= lax.div(place.middle, 2)
+
+    @pl.when(lower)
+    def _():
+        slim.start_by(True)
+
+    @pl.when(lower & hurried)
+    def _():
+        wide.start_by(True)
 
     @pl.when(place.low & place.early)
     def _():
@@ -456,10 +466,9 @@
             wide.wait_corners(dz)
             wide.take_corners(dz)
 
-    @pl.when(place.edge & place.early & jnp.logical_not(place.upper))
-    def _():
-        for exchange in exchanges:
-            exchange.start_by(True)
+    @pl.when(lower & jnp.logical_not(hurried))
+    def _():
+        wide.start_by(True)
 
     @pl.when(place.low & place.early)
     def _():
@@ -555,7 +564,8 @@
     w_self_ref,
     w_tensor_ref,
     w_out_ref,
-    result_ref,
+    energies_ref,
+    forces_ref,
     turned,
     spots,
     scalars,
@@ -567,6 +577,7 @@
     back_rows,
     pulled,
     far_spots,
+    atom_hits,
     sphere_spread,
     self_rows,
     slope_rows,
@@ -754,6 +765,17 @@
     lax.fori_loop(0, PAIRS // FIRST, first_group, 0)
     if stop == 3:
         return
+
+    spots[...] = inner_atom(neighbours)
+    far_spots[...] = inner_atom(centre_rows)
+    atoms = lax.broadcasted_iota(jnp.int32, (64, EDGES), 0).astype(jnp.int16)
+    one, none = jnp.ones((), BF16), jnp.zeros((), BF16)
+    for block in range(BLOCKS):
+        near = jnp.where(atoms == spots[block : block + 1, :].astype(jnp.int16), one, none)
+        far = jnp.where(atoms == far_spots[block : block + 1, :].astype(jnp.int16), one, none)
+        lanes = slice(EDGES * block, EDGES * block + EDGES)
+        atom_hits[0:64, lanes] = far - near
+        atom_hits[64:128, lanes] = far
 
     wide_ready()
     for place in range(4):
@@ -838,33 +860,20 @@
         high, low = split(value)
         pulled[pl.ds(at, BLOCKS, stride=8), :] = high.astype(F32)
         pulled[pl.ds(4 + at, BLOCKS, stride=8), :] = low.astype(F32)
-    spots[...] = inner_atom(neighbours)
-    far_spots[...] = inner_atom(centre_rows)
     if stop == 6:
         return
 
-    def scatter(turn, total):
-        near, far, values = [], [], []
-        atoms = lax.broadcasted_iota(jnp.int32, (64, EDGES), 0).astype(jnp.int16)
-        one, none = jnp.ones((), BF16), jnp.zeros((), BF16)
-        for at in range(SCATTER):
-            block = turn * SCATTER + at
-            spot = spots[pl.ds(block, 1), :].astype(jnp.int16)
-            near.append(jnp.where(atoms == spot, one, none))
-            spot = far_spots[pl.ds(block, 1), :].astype(jnp.int16)
-            far.append(jnp.where(atoms == spot, one, none))
-            values.append(pulled[pl.ds(pl.multiple_of(8 * block, 8), 8), :])
-        near = jnp.concatenate(near, axis=1)
-        far = jnp.concatenate(far, axis=1)
+    total = jnp.zeros((128, 8), F32)
+    for turn in range(BLOCKS // SCATTER):
+        values = [pulled[8 * at : 8 * at + 8, :] for at in range(turn * SCATTER, (turn + 1) * SCATTER)]
         values = jnp.concatenate(values, axis=1).astype(BF16)
-        return total + dot_nt(jnp.concatenate([far - near, far], axis=0), values)
-
-    total = lax.fori_loop(0, BLOCKS // SCATTER, scatter, jnp.zeros((128, 8), F32))
+        lanes = slice(turn * SCATTER * EDGES, (turn + 1) * SCATTER * EDGES)
+        total = total + dot_nt(atom_hits[:, lanes], values)
     total = jnp.concatenate([total, jnp.zeros((128, 120), F32)], axis=1).T
     total = total[0:4] + total[4:8]
     for axis in range(3):
-        result_ref[axis] = total[axis : axis + 1, 0:64]
-    result_ref[3] = total[3:4, 64:128]
+        forces_ref[axis] = total[axis : axis + 1, 0:64]
+    energies_ref[...] = total[3:4, 64:128]
 
 
 def edge_scratch():
@@ -880,6 +889,7 @@
         pltpu.VMEM((24 * BLOCKS, EDGES), F32),
         pltpu.VMEM((8 * BLOCKS, EDGES), F32),
         pltpu.VMEM((BLOCKS, EDGES), jnp.int32),
+        pltpu.VMEM((128, BLOCKS * EDGES), BF16),
         pltpu.VMEM((PAIRS, 80, LANES), BF16),
         pltpu.VMEM((PAIRS, 128, LANES), F32),
         pltpu.VMEM((PAIRS, 128, LANES), F32),
@@ -891,7 +901,7 @@
 
 
 def whole_kernel(features_ref, shifts_ref, *refs):
-    operands, refs = refs[:10], refs[10:]
+    operands, refs = refs[:11], refs[11:]
     slim, wide, by_slim_out, by_wide_out, by_slim_in, by_wide_in = refs[:6]
     corner_slim, corner_wide, packed = refs[6:9]
     by_send, by_recv, send_sem, recv_sem, go = refs[9:HALO_SCRATCH]
@@ -942,9 +952,12 @@
 def whole(*operands):
     return pl.pallas_call(
         whole_kernel,
-        out_shape=jax.ShapeDtypeStruct((4, 1, 64), F32),
+        out_shape=(
+            jax.ShapeDtypeStruct((1, 64), F32),
+            jax.ShapeDtypeStruct((3, 1, 64), F32),
+        ),
         in_specs=[VMEM] * 11,
-        out_specs=VMEM,
+        out_specs=(VMEM, VMEM),
         scratch_shapes=[
             pltpu.VMEM((ROWS, SLIM), BF16),
             pltpu.VMEM((ROWS, WIDE), BF16),
@@ -982,7 +995,7 @@
     w_tensor,
     w_out,
 ):
-    result = whole(
+    energies, forces = whole(
         features.reshape(64, WIDE),
         shifts.reshape(64, 3).T,
         block_counts.reshape(1, 1),
@@ -995,7 +1008,7 @@
         w_tensor,
         w_out.reshape(1, 128),
     )
-    return result[3].reshape(1, 1, 1, 64), result[0:3].reshape(1, 1, 1, 3, 64)
+    return energies.reshape(1, 1, 1, 64), forces.reshape(1, 1, 1, 3, 64)
 
 
 def solution(mesh):

time: 61.7 us -> 61.5 us (level)
  the two profiles are of different devices: /device:TPU:641 before, /device:TPU:1 now
where the time goes in v4:
time: 61.5 us; the launch traced here: 61.3 us
  Pallas kernels  58.3 us (95%)
  local copies, waits for them, and re-layouts  1.69 us (3%)
  between operations  1.3 us (2%)
    pallas_call x1, Pallas kernels, whole(): pl.pallas_call(whole_kernel, out_shape=(jax.ShapeDtypeStruct((1, 64), F32...  58.3 us
    unnamed x6, local copies, waits for them, and re-layouts  1.69 us

profile of v4, /device:TPU:1, one launch (start us, length us, event | category | flops | bytes accessed | tf_op | source)
XLA Modules:
  0.0 61.3 jit_solution(9151914708426623094)
XLA Ops:
  1.3 58.3 %boxes.1 = (f32[1,64]{1,0:T(1,128)}, f32[3,1,64]{2,1,0:T(1,128)}) custom-call(bf16[64,640]{1,0:T(8,128)(2,1)} %bitcast.16, bf16[3,64]{1,0:T(4,128)(2,1)} %bitcast.21, s32[1,1]{1,0:T(1,128)} %bitcast.15.refs_0_, s32[4,48]{1,0:T(4,128)} %bitcast.19, s32[48,128]{1,0:T(8,128)} %bitcast.18, bf16[128,128]{1,0:T(8,128)(2,1)} %refs_3_.1, f32[8,128]{1,0:T(8,128)} %refs_4_.1, ...), custom_call_target="tpu_custom_call" | custom-call | tf_op jit(solution)/shard_map/boxes/pallas_call | solution.py:953
  59.6 0.0 copy-start.1
  59.6 0.0 copy-start
  59.6 0.6 %copy-done.1 = f32[1,64]{1,0:T(1,128)S(1)} copy-done((f32[1,64]{1,0:T(1,128)S(1)}, f32[1,64]{1,0:T(1,128)}, u32[]{:S(2)}) %copy-start.1) | copy-done | bytes 280
  60.3 0.5 copy.17
  60.8 0.0 copy-done
  60.8 0.6 copy.18
Async XLA Ops:
  59.6 0.6 %copy-start.1 = (f32[1,64]{1,0:T(1,128)S(1)}, f32[1,64]{1,0:T(1,128)}, u32[]{:S(2)}) copy-start(f32[1,64]{1,0:T(1,128)} %get-tuple-element.4) | copy-start | bytes 772
  59.6 1.1 %copy-start = (f32[3,1,64]{2,1,0:T(1,128)S(1)}, f32[3,1,64]{2,1,0:T(1,128)}, u32[]{:S(2)}) copy-start(f32[3,1,64]{2,1,0:T(1,128)} %get-tuple-element.5) | copy-start | bytes 2308

commit v5 on v4

--- a/solution.py
+++ b/solution.py
@@ -25,7 +25,7 @@
 BLOCKS = 48
 EDGES = 128
 PAIRS = BLOCKS // 2
-SCATTER = 24
+SCATTER = 12
 GATHER = 24
 FIRST = 24
 SECOND = 12
@@ -430,15 +430,10 @@
 
     slim.spread_by()
     lower = place.edge & place.early & jnp.logical_not(place.upper)
-    hurried = place.bz >= lax.div(place.middle, 2)
 
     @pl.when(lower)
     def _():
         slim.start_by(True)
-
-    @pl.when(lower & hurried)
-    def _():
-        wide.start_by(True)
 
     @pl.when(place.low & place.early)
     def _():
@@ -456,17 +451,21 @@
         slim.wait_corners(1)
         slim.take_corners(1)
 
+    @pl.when(place.low)
+    def _():
+        wide.wait_corners(-1)
+        wide.take_corners(-1)
+
     for side in range(2):
         wide.by_copy(side).wait_recv()
     wide.spread_by()
-    for wraps, dz in ((place.low, -1), (place.high, 1)):
-
-        @pl.when(wraps)
-        def _():
-            wide.wait_corners(dz)
-            wide.take_corners(dz)
-
-    @pl.when(lower & jnp.logical_not(hurried))
+
+    @pl.when(place.high)
+    def _():
+        wide.wait_corners(1)
+        wide.take_corners(1)
+
+    @pl.when(lower)
     def _():
         wide.start_by(True)
 
@@ -863,13 +862,12 @@
     if stop == 6:
         return
 
-    total = jnp.zeros((128, 8), F32)
+    total = jnp.zeros((8, 128), F32)
     for turn in range(BLOCKS // SCATTER):
         values = [pulled[8 * at : 8 * at + 8, :] for at in range(turn * SCATTER, (turn + 1) * SCATTER)]
         values = jnp.concatenate(values, axis=1).astype(BF16)
         lanes = slice(turn * SCATTER * EDGES, (turn + 1) * SCATTER * EDGES)
-        total = total + dot_nt(atom_hits[:, lanes], values)
-    total = jnp.concatenate([total, jnp.zeros((128, 120), F32)], axis=1).T
+        total = total + dot_nt(values, atom_hits[:, lanes])
     total = total[0:4] + total[4:8]
     for axis in range(3):
         forces_ref[axis] = total[axis : axis + 1, 0:64]

time: 61.5 us -> 59.5 us (0.967)
  Pallas kernels: 58.3 us -> 56.3 us
    pallas_call x1, Pallas kernels: 58.3 us -> 56.3 us  [whole(): pl.pallas_call(whole_kernel, out_shape=(jax.ShapeDtypeStruct((1, 64), F32...]
where the time goes in v5:
time: 59.5 us; the launch traced here: 59.3 us
  Pallas kernels  56.3 us (95%)
  local copies, waits for them, and re-layouts  1.69 us (3%)
  between operations  1.3 us (2%)
    pallas_call x1, Pallas kernels, whole(): pl.pallas_call(whole_kernel, out_shape=(jax.ShapeDtypeStruct((1, 64), F32...  56.3 us
    unnamed x6, local copies, waits for them, and re-layouts  1.69 us

profile of v5, /device:TPU:1, one launch (start us, length us, event | category | flops | bytes accessed | tf_op | source)
XLA Modules:
  0.0 59.3 jit_solution(13293685454878853746)
XLA Ops:
  1.3 56.3 %boxes.1 = (f32[1,64]{1,0:T(1,128)}, f32[3,1,64]{2,1,0:T(1,128)}) custom-call(bf16[64,640]{1,0:T(8,128)(2,1)} %bitcast.16, bf16[3,64]{1,0:T(4,128)(2,1)} %bitcast.21, s32[1,1]{1,0:T(1,128)} %bitcast.15.refs_0_, s32[4,48]{1,0:T(4,128)} %bitcast.19, s32[48,128]{1,0:T(8,128)} %bitcast.18, bf16[128,128]{1,0:T(8,128)(2,1)} %refs_3_.1, f32[8,128]{1,0:T(8,128)} %refs_4_.1, ...), custom_call_target="tpu_custom_call" | custom-call | tf_op jit(solution)/shard_map/boxes/pallas_call | solution.py:951
  57.6 0.0 copy-start.1
  57.6 0.0 copy-start
  57.6 0.6 %copy-done.1 = f32[1,64]{1,0:T(1,128)S(1)} copy-done((f32[1,64]{1,0:T(1,128)S(1)}, f32[1,64]{1,0:T(1,128)}, u32[]{:S(2)}) %copy-start.1) | copy-done | bytes 280
  58.2 0.5 copy.17
  58.8 0.0 copy-done
  58.8 0.6 copy.18
Async XLA Ops:
  57.6 0.6 %copy-start.1 = (f32[1,64]{1,0:T(1,128)S(1)}, f32[1,64]{1,0:T(1,128)}, u32[]{:S(2)}) copy-start(f32[1,64]{1,0:T(1,128)} %get-tuple-element.4) | copy-start | bytes 772
  57.6 1.1 %copy-start = (f32[3,1,64]{2,1,0:T(1,128)S(1)}, f32[3,1,64]{2,1,0:T(1,128)}, u32[]{:S(2)}) copy-start(f32[3,1,64]{2,1,0:T(1,128)} %get-tuple-element.5) | copy-start | bytes 2308
